TPU v7x, 32 devices: a whole 2x2x4 slice. The times are simulated.
32 devices in a mesh: group: 2 (over y), replica: 8 (over z, x), tensor: 2 (over core).
Axes of the slice: x: 2, y: 2, z: 4, core: 2. Of those that a mesh axis runs over, the one named last changes fastest.
Arguments:
- hidden: bfloat16 [1536, 1, 4096], P(('group', 'replica'), None, 'tensor'), parts along dimension 0, may hold values from -6 to 6
- queries: bfloat16 [1536, 1, 4, 1024], P(('group', 'replica'), None, 'tensor'), parts along dimension 0, may hold values from -200 to 200
- incoming_keys: bfloat16 [1536, 1, 4, 128], P(('group', 'replica'), None, 'tensor'), parts along dimension 0, may hold values from -6 to 6
- stored_key_cache: bfloat16 [1536, 4, 16, 128], P(('group', 'replica'), 'tensor'), parts along dimension 0, may hold values from -6 to 6
- stored_value_cache: bfloat16 [1536, 4, 16, 128], P(('group', 'replica'), 'tensor'), parts along dimension 0, may hold values from -6 to 6
- base_value_weight: bfloat16 [4096, 512], P('tensor'), may hold values from -0.09375 to 0.09375
- adapter_down_rows: bfloat16 [8, 64, 4096], P('replica', None, 'tensor'), may hold values from -0.09375 to 0.09375
- adapter_up_rows: bfloat16 [8, 64, 512], P('replica', None, 'tensor'), may hold values from -0.75 to 0.75
- request_adapter: int32 [768], P('replica'), may hold values from 0 to 7, as said below
- adapter_replica: int32 [8], replicated, may hold values from 0 to 7, as said below
- replica_slot_count: int32 [8], P('replica'), may hold values from 84 to 96, as said below
- cache_length: int32 [768], P('replica'), may hold values from 2 to 16, as said below
Outputs:
- attention: bfloat16 [1536, 1, 4, 1024], P(('group', 'replica'), None, 'tensor'), parts along dimension 0
- new_values: bfloat16 [1536, 1, 4, 128], P(('group', 'replica'), None, 'tensor'), parts along dimension 0
There are 2 independent parts, one for each index of `group`. A program takes and returns all parts, laid end to end along the dimension named above; an argument that names none is the same for every part. Nothing has to cross between parts.
Inputs may be any that keep to these rules, and one draw needn't show every extreme that they name: `request_adapter`: among the slots of one replica at most 24 have adapters of one home, and some home has 24 in every replica's first 24 slots. `adapter_replica`: A permutation. `replica_slot_count`: slots 0 to load - 1 of a replica are live; some replica is full. `cache_length`: some slot uses all 16 positions.
All inputs are finite; a program needn't handle non-finite values.
Results may differ from a plain program's by a relative error of at most 0.0053.
Values may be sent and summed in bfloat16 or wider, within the bound.
No kernel may reach another device: no remote copies, remote signals or barrier semaphores. Data moves between devices by JAX's collectives and lax.ppermute only.
A program may use at most 64 MiB of HBM per device.

v0:
```python
import math

import jax
import jax.numpy as jnp
from jax import lax
from jax.sharding import PartitionSpec as P


def attend(query_rows, fresh_keys, cached_keys, cached_values, fresh_values, lengths):
    row_count, step_count, head_count, query_width = query_rows.shape
    head_size = cached_keys.shape[3]
    grouped = query_rows.reshape(
        row_count, step_count, head_count, query_width // head_size, head_size
    )
    score_scale = 1.0 / math.sqrt(head_size)
    cache_scores = (
        jnp.einsum("rsghd,rgpd->rsghp", grouped, cached_keys, preferred_element_type=jnp.float32)
        * score_scale
    )
    fresh_scores = (
        jnp.einsum("rsghd,rjgd->rsghj", grouped, fresh_keys, preferred_element_type=jnp.float32)
        * score_scale
    )
    places = jnp.arange(cached_keys.shape[2], dtype=jnp.int32)
    cache_valid = places[None, :] < lengths[:, None]
    step_index = jnp.arange(step_count, dtype=jnp.int32)
    step_valid = step_index[None, :] <= step_index[:, None]
    cache_scores = jnp.where(cache_valid[:, None, None, None, :], cache_scores, -1e30)
    fresh_scores = jnp.where(step_valid[None, :, None, None, :], fresh_scores, -1e30)
    row_max = jnp.maximum(jnp.max(cache_scores, axis=-1), jnp.max(fresh_scores, axis=-1))[..., None]
    cache_exp = jnp.exp(cache_scores - row_max)
    fresh_exp = jnp.exp(fresh_scores - row_max)
    totals = jnp.sum(cache_exp, axis=-1, keepdims=True) + jnp.sum(fresh_exp, axis=-1, keepdims=True)
    cache_weights = (cache_exp / totals).astype(jnp.bfloat16)
    fresh_weights = (fresh_exp / totals).astype(jnp.bfloat16)
    mixed = jnp.einsum(
        "rsghp,rgpd->rsghd", cache_weights, cached_values, preferred_element_type=jnp.float32
    )
    mixed = mixed + jnp.einsum(
        "rsghj,rjgd->rsghd", fresh_weights, fresh_values, preferred_element_type=jnp.float32
    )
    return mixed.reshape(row_count, step_count, head_count, query_width).astype(jnp.bfloat16)


def local(
    hidden,
    queries,
    incoming_keys,
    stored_key_cache,
    stored_value_cache,
    base_value_weight,
    adapter_down_rows,
    adapter_up_rows,
    request_adapter,
    adapter_replica,
    replica_slot_count,
    cache_length,
):
    slot_count, step_count, feature_half = hidden.shape
    replicas = lax.axis_size("replica")
    capacity = max(2, 2 * slot_count // replicas)
    adapter_count = adapter_replica.shape[0]
    heads_here = stored_key_cache.shape[1]
    head_size = stored_key_cache.shape[3]
    column_count = heads_here * head_size
    matches = request_adapter[:, None] == jnp.arange(adapter_count, dtype=jnp.int32)[None, :]
    homes = jnp.sum(jnp.where(matches, adapter_replica[None, :], 0), axis=1)
    slot_index = jnp.arange(slot_count, dtype=jnp.int32)
    live_mask = slot_index < replica_slot_count[0]
    earlier = (
        (homes[:, None] == homes[None, :])
        & live_mask[None, :]
        & (slot_index[None, :] < slot_index[:, None])
    )
    position = jnp.sum(earlier.astype(jnp.int32), axis=1)
    target = jnp.where(live_mask, homes * capacity + position, replicas * capacity)
    outgoing = jnp.zeros((replicas * capacity, step_count, feature_half), jnp.bfloat16)
    outgoing = (
        outgoing.at[target]
        .set(hidden, mode="drop")
        .reshape(replicas, capacity, step_count, feature_half)
    )
    down_matrix = adapter_down_rows[0]
    up_matrix = adapter_up_rows[0]
    partial_rank = jnp.einsum(
        "ncsd,qd->ncsq",
        lax.all_to_all(outgoing, "replica", split_axis=0, concat_axis=0, tiled=True),
        down_matrix,
        preferred_element_type=jnp.float32,
    )
    summed_rank = lax.psum(partial_rank, "tensor")
    shrunk = summed_rank.astype(jnp.bfloat16)
    home_delta = jnp.einsum("ncsq,qe->ncse", shrunk, up_matrix, preferred_element_type=jnp.float32)
    returned_rows = lax.all_to_all(home_delta, "replica", split_axis=0, concat_axis=0, tiled=True)
    flattened = returned_rows.reshape(replicas * capacity, step_count, column_count)
    delta = jnp.take(flattened, target, axis=0, mode="clip")
    base_part = jnp.dot(
        hidden.reshape(slot_count * step_count, feature_half),
        base_value_weight,
        preferred_element_type=jnp.float32,
    )
    base_part = base_part.reshape(slot_count, step_count, base_value_weight.shape[1])
    base_total = lax.psum(base_part, "tensor")
    own_heads = lax.dynamic_slice_in_dim(
        base_total, lax.axis_index("tensor") * column_count, column_count, 2
    )
    fresh_values = jnp.where(live_mask[:, None, None], own_heads + delta, 0.0).astype(jnp.bfloat16)
    fresh_values = fresh_values.reshape(slot_count, step_count, heads_here, head_size)
    mixed = attend(
        queries, incoming_keys, stored_key_cache, stored_value_cache, fresh_values, cache_length
    )
    mixed = jnp.where(live_mask[:, None, None, None], mixed, jnp.zeros_like(mixed))
    return (mixed, fresh_values)


def solution(mesh):
    placed = (
        P(("group", "replica"), None, "tensor"),
        P(("group", "replica"), None, "tensor", None),
        P(("group", "replica"), None, "tensor", None),
        P(("group", "replica"), "tensor", None, None),
        P(("group", "replica"), "tensor", None, None),
        P("tensor", None),
        P("replica", None, "tensor"),
        P("replica", None, "tensor"),
        P("replica"),
        P(),
        P("replica"),
        P("replica"),
    )
    return jax.shard_map(
        local,
        mesh=mesh,
        in_specs=placed,
        out_specs=(
            P(("group", "replica"), None, "tensor", None),
            P(("group", "replica"), None, "tensor", None),
        ),
        check_vma=False,
    )
```

profile of v0, /device:TPU:0, one launch (start us, length us, event | category | flops | bytes accessed | tf_op | source)
XLA Modules:
  0.0 69.5 jit_solution(13309774803326369219)
XLA Ops:
  7.2 0.0 copy-start
  7.2 0.0 copy-start.1
  8.0 0.8 %select_reduce_fusion = s32[96]{0:T(128)S(1)} fusion(s32[8]{0:T(128)} %param.21, s32[96]{0:T(128)} %param.20), kind=kLoop, calls=%fused_computation.43 | loop fusion | flops 2208 | bytes 800 | tf_op jit(solution)/shard_map/reduce_sum | solution.py:67
  8.8 0.2 convert_reduce_fusion
  8.9 2.6 %scatter_custom_fusion = bf16[192,2048]{1,0:T(8,128)(2,1)} fusion(s32[96]{0:T(128)S(1)} %get-tuple-element.12, bf16[96,1,2048]{2,0,1:T(8,128)(2,1)} %param.12, bf16[]{:T(256)} %constant.4.clone.1), kind=kCustom, calls=%fused_computation.18 | custom fusion | bytes 1179650 | tf_op jit(solution)/shard_map/scatter | solution.py:80
  11.6 7.3 %all-to-all-start = ((bf16[8,24,1,2048]{3,1,2,0:T(8,128)(2,1)}), bf16[8,24,1,2048]{3,1,2,0:T(8,128)(2,1)S(1)}, u32[]{:S(2)}, u32[]{:S(2)}) async-start(bf16[8,24,1,2048]{3,1,2,0:T(8,128)(2,1)} %bitcast.102), calls=%async_computation | async-start | bytes 1572864 | tf_op jit(solution)/shard_map/all_to_all | solution.py:87
  18.8 0.0 copy-start.3
  18.8 0.0 all-reduce.2.cloned.1.call-start
  18.9 0.0 copy-done
  18.9 0.0 copy-done.1
  18.9 1.1 %convolution_bitcast_fusion.1 = f32[96,1,512]{2,0,1:T(8,128)} fusion(bf16[2048,512]{1,0:T(8,128)(2,1)S(1)} %copy-done, bf16[96,1,2048]{2,0,1:T(8,128)(2,1)S(1)} %copy-done.1), kind=kOutput, calls=%fused_computation.10 | convolution fusion | flops 201326592 | bytes 2686976 | tf_op jit(solution)/shard_map/dot_general | solution.py:97
  20.0 0.0 copy-start.4
  20.0 0.0 all-reduce.2.cloned.1.call-update
  20.1 1.2 %reshape.200 = bf16[96,2,8,128]{3,2,1,0:T(8,128)(2,1)S(1)} reshape(bf16[96,1,2,1024]{3,2,1,0:T(2,128)(2,1)} %param.13) | data formatting | bytes 786432 | tf_op jit(solution)/shard_map/reshape.2
  21.3 0.0 copy-done.3
  21.3 0.1 iota_compare_fusion.1
  21.4 0.0 copy-start.2
  21.4 2.6 %fusion.27 = (f32[96,2,8]{2,1,0:T(2,128)S(1)}, f32[96,1,2,8,16]{4,3,2,0,1:T(8,128)}) fusion(bf16[96,2,16,128]{3,2,1,0:T(8,128)(2,1)} %param.15, bf16[96,2,8,128]{3,2,1,0:T(8,128)(2,1)S(1)} %reshape.200, pred[96,16]{1,0:T(8,128)(4,1)S(1)} %iota_compare_fusion.1), kind=kOutput, calls=%fused_computation.50 | convolution fusion | flops 6363648 | bytes 1285632 | tf_op jit(solution)/shard_map/rsghd,rgpd->rsghp/dot_general | solution.py:17
  24.0 0.1 copy.28
  24.1 0.0 copy-done.4
  24.1 0.4 fusion.17
  24.4 0.1 copy.37
  24.5 0.1 copy.29
  24.7 14.3 %all-to-all-done = bf16[8,24,1,2048]{3,1,2,0:T(8,128)(2,1)S(1)} async-done(((bf16[8,24,1,2048]{3,1,2,0:T(8,128)(2,1)}), bf16[8,24,1,2048]{3,1,2,0:T(8,128)(2,1)S(1)}, u32[]{:S(2)}, u32[]{:S(2)}) %all-to-all-start) | async-done | bytes 786464 | tf_op jit(solution)/shard_map/all_to_all | solution.py:87
  39.0 1.3 %convolution_bitcast_fusion.3 = f32[8,24,1,64]{3,1,0,2:T(8,128)S(1)} fusion(bf16[8,24,1,2048]{3,1,2,0:T(8,128)(2,1)S(1)} %all-to-all-done, bf16[1,64,2048]{2,1,0:T(8,128)(2,1)} %param.18), kind=kOutput, calls=%fused_computation.12 | convolution fusion | flops 50331648 | bytes 1097728 | tf_op jit(solution)/shard_map/ncsd,qd->ncsq/dot_general | solution.py:85
  40.3 3.7 %psum.15 = bf16[8,24,1,64]{3,1,0,2:T(8,128)(2,1)S(1)} all-reduce(f32[8,24,1,64]{3,1,0,2:T(8,128)S(1)} %convolution_bitcast_fusion.3), channel_id=1, replica_groups=mesh['group'=2,'replica'=8,'tensor'=2] {'tensor'}, use_global_device_ids=true, to_apply=%region_6.7 | all-reduce | flops 12288 | bytes 73728 | tf_op jit(solution)/shard_map/psum | solution.py:91
  44.0 0.0 copy-done.2
  44.0 0.8 %convolution_bitcast_fusion.2 = f32[8,24,1,256]{3,1,2,0:T(8,128)} fusion(bf16[8,24,1,64]{3,1,0,2:T(8,128)(2,1)S(1)} %psum.15, bf16[1,64,256]{2,1,0:T(8,128)(2,1)S(1)} %copy-done.2), kind=kOutput, calls=%fused_computation.11 | convolution fusion | flops 6291456 | bytes 253952 | tf_op jit(solution)/shard_map/ncsq,qe->ncse/dot_general | solution.py:93
  44.9 3.6 %all-to-all-start.1 = ((f32[8,24,1,256]{3,1,2,0:T(8,128)}), f32[8,24,1,256]{3,1,2,0:T(8,128)S(1)}, u32[]{:S(2)}, u32[]{:S(2)}) async-start(f32[8,24,1,256]{3,1,2,0:T(8,128)} %convolution_bitcast_fusion.2), calls=%async_computation.1 | async-start | bytes 393216 | tf_op jit(solution)/shard_map/all_to_all | solution.py:94
  48.4 1.7 %fusion.7 = f32[96,2,8]{2,1,0:T(2,128)S(1)} fusion(f32[96,1,2,8,16]{4,3,2,0,1:T(8,128)} %get-tuple-element.17, f32[96,2,8]{2,1,0:T(2,128)S(1)} %copy.29), kind=kLoop, calls=%fused_computation.17 | loop fusion | flops 47616 | bytes 110592 | tf_op jit(solution)/shard_map/reduce_sum | solution.py:33
  50.1 0.1 copy.30
  50.2 0.1 copy.31
  50.3 0.1 copy.33
  50.5 6.5 %all-to-all-done.1 = f32[8,24,1,256]{3,1,2,0:T(8,128)S(1)} async-done(((f32[8,24,1,256]{3,1,2,0:T(8,128)}), f32[8,24,1,256]{3,1,2,0:T(8,128)S(1)}, u32[]{:S(2)}, u32[]{:S(2)}) %all-to-all-start.1) | async-done | bytes 196640 | tf_op jit(solution)/shard_map/all_to_all | solution.py:94
  56.9 0.7 %gather_fusion = f32[96,256]{1,0:T(8,128)S(1)} fusion(f32[192,256]{1,0:T(8,128)S(1)} %bitcast.101, s32[1024]{0:T(1024)S(1)} %pad_clamp_fusion), kind=kCustom, calls=%fused_computation | custom fusion | bytes 196992 | tf_op jit(solution)/shard_map/jit(_take)/gather | solution.py:96
  57.6 0.0 all-reduce.2.cloned.1.call-done
  57.7 1.0 %fusion.16 = bf16[96,1,256]{2,0,1:T(8,128)(2,1)S(1)} fusion(f32[96,256]{1,0:T(8,128)S(1)} %gather_fusion, f32[96,1,512]{2,0,1:T(8,128)} %all-reduce.2.cloned.1.call-done, s32[]{:T(128)S(6)} %select_n.60, pred[96]{0:T(512)(128)(4,1)S(1)} %iota_compare_fusion.3), kind=kLoop, calls=%fused_computation.27 | loop fusion | flops 73728 | bytes 245860 | tf_op jit(solution)/shard_map/convert_element_type | solution.py:107
  58.7 0.1 reshape.211
  58.7 0.6 reshape.210
  59.4 2.0 %fusion.5 = bf16[96,1,2,8,128]{4,3,2,0,1:T(8,128)(2,1)S(1)} fusion(bf16[96,2,16,128]{3,2,1,0:T(8,128)(2,1)} %param.16, f32[96,2,8]{2,1,0:T(2,128)S(1)} %copy.33, f32[96,2,128]{2,1,0:T(2,128)S(1)} %reshape.211, f32[96,1,2,8,16]{4,3,2,0,1:T(8,128)} %get-tuple-element.17, f32[96,2,8]{2,1,0:T(2,128)S(1)} %copy.31, f32[96,2,8]{2,1,0:T(2,128)S(1)} %copy.29), kind=kOutput, calls=%fused_computation.9 | convolution fusion | flops 6955008 | bytes 1394688 | tf_op jit(solution)/shard_map/rsghp,rgpd->rsghd/dot_general | solution.py:36
  61.4 0.1 convert_element_type.44
  61.5 1.2 %broadcast_select_fusion = bf16[96,1,2,1024]{3,2,1,0:T(2,128)(2,1)} fusion(pred[96]{0:T(512)(128)(4,1)S(1)} %iota_compare_fusion.3, bf16[96,1,2,1024]{3,2,0,1:T(2,128)(2,1)S(1)} %convert_element_type.44), kind=kLoop, calls=%fused_computation.16 | loop fusion | flops 196608 | bytes 786528 | tf_op jit(solution)/shard_map/jit(_where)/select_n | solution.py:112
  (5 shorter events, 0.0 us)
Async XLA Ops:
  7.2 11.7 %copy-start = (bf16[2048,512]{1,0:T(8,128)(2,1)S(1)}, bf16[2048,512]{1,0:T(8,128)(2,1)}, u32[]{:S(2)}) copy-start(bf16[2048,512]{1,0:T(8,128)(2,1)} %param.17) | copy-start | bytes 6291460
  7.2 11.7 %copy-start.1 = (bf16[96,1,2048]{2,0,1:T(8,128)(2,1)S(1)}, bf16[96,1,2048]{2,0,1:T(8,128)(2,1)}, u32[]{:S(2)}) copy-start(bf16[96,1,2048]{2,0,1:T(8,128)(2,1)} %param.12) | copy-start | bytes 1179652
  11.6 27.4 %all-to-all-start = ((bf16[8,24,1,2048]{3,1,2,0:T(8,128)(2,1)}), bf16[8,24,1,2048]{3,1,2,0:T(8,128)(2,1)S(1)}, u32[]{:S(2)}, u32[]{:S(2)}) async-start(bf16[8,24,1,2048]{3,1,2,0:T(8,128)(2,1)} %bitcast.102), calls=%async_computation | async-start | bytes 1572864 | tf_op jit(solution)/shard_map/all_to_all | solution.py:87
  18.8 2.5 %copy-start.3 = (s32[96]{0:T(128)S(1)}, s32[96]{0:T(128)}, u32[]{:S(2)}) copy-start(s32[96]{0:T(128)} %param.23) | copy-start | bytes 1156
  18.8 38.9 %all-reduce.2.cloned.1.call-start = ((), (), s32[]{:S(2)}) async-start(), calls=%async_computation.2 | async-start | bytes 393216 | tf_op jit(solution)/shard_map/psum | solution.py:103
  20.0 4.0 %copy-start.4 = (bf16[96,1,2,128]{3,2,1,0:T(2,128)(2,1)S(1)}, bf16[96,1,2,128]{3,2,1,0:T(2,128)(2,1)}, u32[]{:S(2)}) copy-start(bf16[96,1,2,128]{3,2,1,0:T(2,128)(2,1)} %param.14) | copy-start | bytes 147460
  21.4 22.6 %copy-start.2 = (bf16[1,64,256]{2,1,0:T(8,128)(2,1)S(1)}, bf16[1,64,256]{2,1,0:T(8,128)(2,1)}, u32[]{:S(2)}) copy-start(bf16[1,64,256]{2,1,0:T(8,128)(2,1)} %param.19) | copy-start | bytes 98308
  44.9 12.1 %all-to-all-start.1 = ((f32[8,24,1,256]{3,1,2,0:T(8,128)}), f32[8,24,1,256]{3,1,2,0:T(8,128)S(1)}, u32[]{:S(2)}, u32[]{:S(2)}) async-start(f32[8,24,1,256]{3,1,2,0:T(8,128)} %convolution_bitcast_fusion.2), calls=%async_computation.1 | async-start | bytes 393216 | tf_op jit(solution)/shard_map/all_to_all | solution.py:94
Sparse Core Ops, SparseCore 0:
  22.0 19.4 all-reduce.1
where the time goes:
time: 70.1 us; the launch traced here: 69.5 us
  waiting for transfers between devices  20.8 us (30%)
  between operations  15 us (21%)
  starting transfers between devices  10.8 us (15%)
  matrix products  8.28 us (12%)
  local copies, waits for them, and re-layouts  5.96 us (9%)
  other arithmetic  4.9 us (7%)
  blocking collectives  3.69 us (5%)
    all_to_all x1, waiting for transfers between devices, local(): lax.all_to_all(outgoing, 'replica', split_axis=0, concat_axis=0, tiled=True)  14.3 us
    all_to_all x1, starting transfers between devices, local(): lax.all_to_all(outgoing, 'replica', split_axis=0, concat_axis=0, tiled=True)  7.25 us
    all_to_all x1, waiting for transfers between devices, local(): lax.all_to_all(home_delta, 'replica', split_axis=0, concat_axis=0, tiled=...  6.46 us
    psum x1, blocking collectives, local(): summed_rank = lax.psum(partial_rank, 'tensor')  3.69 us
    all_to_all x1, starting transfers between devices, local(): lax.all_to_all(home_delta, 'replica', split_axis=0, concat_axis=0, tiled=...  3.55 us
    scatter x1, local copies, waits for them, and re-layouts, local(): outgoing = outgoing.at[target].set(hidden, mode='drop').reshape(replicas,...  2.61 us
    dot_general x1, matrix products, attend(): jnp.einsum('rsghd,rgpd->rsghp', grouped, cached_keys, preferred_element_t...  2.59 us
    dot_general x1, matrix products, attend(): jnp.einsum('rsghp,rgpd->rsghd', cache_weights, cached_values, preferred_e...  2.05 us
  transfers between devices with their start and end apart: 3, of which 2 were waited for; matrix products, arithmetic and copies ran while one was open for 15% of the time, Pallas kernels for 0%

commit v1 on v0

v1 whole, which is shorter than its diff:
```python
import functools
import math

import jax
import jax.numpy as jnp
from jax import lax
from jax.experimental import pallas as pl
from jax.experimental.pallas import tpu as pltpu
from jax.sharding import PartitionSpec as P

NEGATIVE = -1e30
GATHER_BYTES = 1 << 22


def swap(array, axis, bit):
    size = lax.axis_size(axis)
    return lax.ppermute(array, axis, [(i, i ^ bit) for i in range(size)])


def cached_kernel(dims, lengths_ref, scalars_ref, hidden_ref, weight_ref, query_ref, key_ref, fresh_ref, value_ref,
                  kept_ref, sent_ref, mixed_ref, share_ref, total_ref):
    heads, query_heads, context, group, steps, scale = dims
    step = pl.program_id(0)
    product = jnp.dot(hidden_ref[...], weight_ref[...], preferred_element_type=jnp.float32)

    @pl.when(step == 0)
    def _():
        total_ref[...] = product

    @pl.when(step > 0)
    def _():
        total_ref[...] += product

    @pl.when(step == steps - 1)
    def _():
        columns = kept_ref.shape[1]
        low, high = total_ref[:, :columns], total_ref[:, columns:]
        first = scalars_ref[1] == 0
        kept_ref[...] = jnp.where(first, low, high)
        sent_ref[...] = jnp.where(first, high, low)

    slots = group // heads
    rows, places = group * query_heads, group * context
    blocks = query_ref.shape[0] // rows
    contract = (((1,), (1,)), ((), ()))

    def pair_of(shape):
        row = lax.broadcasted_iota(jnp.int32, shape, 0)
        return row // (heads * query_heads) * heads + row % heads

    own = pair_of((rows, places)) == lax.broadcasted_iota(jnp.int32, (rows, places), 1) // context
    lane = lax.broadcasted_iota(jnp.int32, (1, places), 1)
    query = query_ref[...]
    fresh = lax.dot_general(query, fresh_ref[...], contract, preferred_element_type=jnp.float32) * scale
    own_fresh = pair_of(fresh.shape) == lax.broadcasted_iota(jnp.int32, fresh.shape, 1)
    fresh = jnp.sum(jnp.where(own_fresh, fresh, 0.0), axis=1, keepdims=True)
    scores = []
    for block in range(blocks):
        base = (step * blocks + block) * slots
        keys = key_ref[pl.ds(block * places, places), :]
        score = lax.dot_general(
            query[block * rows : (block + 1) * rows], keys, contract, preferred_element_type=jnp.float32
        )
        limit = jnp.full((1, places), lengths_ref[base], jnp.int32)
        for s in range(1, slots):
            limit = jnp.where(lane // (heads * context) == s, lengths_ref[base + s], limit)
        scores.append(jnp.where(own & (lane % context < limit), score * scale, NEGATIVE))
    scores = jnp.concatenate(scores, axis=0)
    top = jnp.maximum(jnp.max(scores, axis=1, keepdims=True), fresh)
    parts = jnp.exp(scores - top)
    fresh_part = jnp.exp(fresh - top)
    inverse = 1.0 / (jnp.sum(parts, axis=1, keepdims=True) + fresh_part)
    row_slot = lax.broadcasted_iota(jnp.int32, inverse.shape, 0) // (heads * query_heads)
    inverse = jnp.where(step * blocks * slots + row_slot < scalars_ref[0], inverse, 0.0)
    weights = (parts * inverse).astype(jnp.bfloat16)
    mixed = [
        jnp.dot(
            weights[block * rows : (block + 1) * rows],
            value_ref[pl.ds(block * places, places), :],
            preferred_element_type=jnp.float32,
        )
        for block in range(blocks)
    ]
    mixed_ref[...] = jnp.concatenate(mixed, axis=0)
    share_ref[...] = jnp.where(own_fresh, fresh_part * inverse, 0.0).astype(share_ref.dtype)


def base_and_cached(rows, weight, query_rows, fresh_keys, cached_keys, cached_values, lengths, scalars):
    slots, features = rows.shape
    heads, context, size = cached_keys.shape[1:]
    query_heads = query_rows.shape[0] // (slots * heads)
    group, steps = 8, 4
    columns = weight.shape[1] // 2
    pairs = slots * heads
    dims = (heads, query_heads, context, group, steps, 1.0 / math.sqrt(size))
    return pl.pallas_call(
        functools.partial(cached_kernel, dims),
        grid_spec=pltpu.PrefetchScalarGridSpec(
            num_scalar_prefetch=2,
            grid=(steps,),
            in_specs=[
                pl.BlockSpec((slots, features // steps), lambda i, *_: (0, i)),
                pl.BlockSpec((features // steps, 2 * columns), lambda i, *_: (i, 0)),
                pl.BlockSpec((pairs * query_heads // steps, size), lambda i, *_: (i, 0)),
                pl.BlockSpec((pairs * context // steps, size), lambda i, *_: (i, 0)),
                pl.BlockSpec((pairs // steps, size), lambda i, *_: (i, 0)),
                pl.BlockSpec((pairs * context // steps, size), lambda i, *_: (i, 0)),
            ],
            out_specs=[
                pl.BlockSpec((slots, columns), lambda i, *_: (0, 0)),
                pl.BlockSpec((slots, columns), lambda i, *_: (0, 0)),
                pl.BlockSpec((pairs * query_heads // steps, size), lambda i, *_: (i, 0)),
                pl.BlockSpec((pairs * query_heads // steps, pairs // steps), lambda i, *_: (i, 0)),
            ],
            scratch_shapes=[pltpu.VMEM((slots, 2 * columns), jnp.float32)],
        ),
        out_shape=[
            jax.ShapeDtypeStruct((slots, columns), jnp.float32),
            jax.ShapeDtypeStruct((slots, columns), jnp.float32),
            jax.ShapeDtypeStruct(query_rows.shape, jnp.float32),
            jax.ShapeDtypeStruct((query_rows.shape[0], pairs // steps), jnp.bfloat16),
        ],
        compiler_params=pltpu.CompilerParams(vmem_limit_bytes=56 << 20),
        cost_estimate=pl.CostEstimate(flops=1 << 28, bytes_accessed=12 << 20, transcendentals=1 << 18),
    )(
        lengths,
        scalars,
        rows,
        weight,
        query_rows,
        cached_keys.reshape(pairs * context, size),
        fresh_keys.reshape(pairs, size),
        cached_values.reshape(pairs * context, size),
    )


def final_kernel(count_ref, own_ref, returned_ref, mixed_ref, share_ref, attention_ref, values_ref, spread_ref):
    slots = own_ref.shape[0]
    pairs, size = values_ref.shape
    heads = pairs // slots
    live = lax.broadcasted_iota(jnp.int32, (slots, 1), 0) < count_ref[0]
    fresh = jnp.where(live, own_ref[...] + returned_ref[...].astype(jnp.float32), 0.0)
    for head in range(heads):
        spread_ref[pl.ds(head, slots, stride=heads), :] = fresh[:, head * size : (head + 1) * size]
    values = spread_ref[...].astype(jnp.bfloat16)
    values_ref[...] = values
    group = share_ref.shape[1]
    rows = group * attention_ref.shape[0] // pairs
    for block in range(pairs // group):
        part = pl.ds(block * rows, rows)
        fresh_part = jnp.dot(
            share_ref[part, :], values[block * group : (block + 1) * group], preferred_element_type=jnp.float32
        )
        attention_ref[part, :] = (mixed_ref[part, :] + fresh_part).astype(attention_ref.dtype)


def finish(own, returned, mixed, share, live_count):
    slots, columns = own.shape
    size = mixed.shape[1]
    pairs = slots * columns // size
    vmem = pl.BlockSpec(memory_space=pltpu.VMEM)
    return pl.pallas_call(
        final_kernel,
        in_specs=[pl.BlockSpec(memory_space=pltpu.SMEM), vmem, vmem, vmem, vmem],
        out_specs=[vmem, vmem],
        out_shape=[
            jax.ShapeDtypeStruct(mixed.shape, jnp.bfloat16),
            jax.ShapeDtypeStruct((pairs, size), jnp.bfloat16),
        ],
        scratch_shapes=[pltpu.VMEM((pairs, size), jnp.float32)],
        compiler_params=pltpu.CompilerParams(vmem_limit_bytes=8 << 20),
    )(live_count, own, returned, mixed, share)


def moved_delta(rows, down, up, homes, live_mask):
    slots, features = rows.shape
    replicas = lax.axis_size("replica")
    capacity = max(2, 2 * slots // replicas)
    index = jnp.arange(slots, dtype=jnp.int32)
    earlier = (homes[:, None] == homes[None, :]) & live_mask[None, :] & (index[None, :] < index[:, None])
    position = jnp.sum(earlier.astype(jnp.int32), axis=1)
    target = jnp.where(live_mask, homes * capacity + position, replicas * capacity)
    outgoing = jnp.zeros((replicas * capacity, features), jnp.bfloat16).at[target].set(rows, mode="drop")
    arrived = lax.all_to_all(outgoing, "replica", split_axis=0, concat_axis=0, tiled=True)
    part = jnp.einsum("nd,qd->nq", arrived, down, preferred_element_type=jnp.float32)
    shrunk = lax.psum(part, "tensor").astype(jnp.bfloat16)
    delta = jnp.dot(shrunk, up, preferred_element_type=jnp.float32)
    returned = lax.all_to_all(delta, "replica", split_axis=0, concat_axis=0, tiled=True)
    return jnp.take(returned, target, axis=0, mode="clip")


def rank_kernel(offsets, half, ids_ref, rows_ref, other_ref, homes_ref, other_homes_ref, down_ref, *rest):
    mine, theirs = rest[: len(offsets) - 1], rest[len(offsets) - 1 : -2]
    ranks_ref, panel_ref = rest[-2:]
    rank = 2 * half
    panel_ref[pl.ds(0, rank), :] = down_ref[...]
    for k in range(1, len(offsets)):
        at = pl.multiple_of(k * rank + ids_ref[0], half)
        panel_ref[pl.ds(at, half), :] = mine[k - 1][...]
        at = pl.multiple_of(k * rank + half - ids_ref[0], half)
        panel_ref[pl.ds(at, half), :] = theirs[k - 1][...]
    contract = (((1,), (1,)), ((), ()))
    for i, (rows, homes) in enumerate(((rows_ref, homes_ref), (other_ref, other_homes_ref))):
        product = lax.dot_general(panel_ref[...], rows[...], contract, preferred_element_type=jnp.float32)
        total = jnp.zeros((rank, product.shape[1]), jnp.float32)
        for k in range(len(offsets)):
            here = homes[...] == ids_ref[1 + k]
            total += jnp.where(here, product[k * rank : (k + 1) * rank], 0.0)
        ranks_ref[pl.ds(i * rank, rank), :] = total


def delta_kernel(count, ids_ref, homes_ref, other_homes_ref, ranks_ref, got_ref, kept_ref, base_ref, *rest):
    ups = rest[:count]
    own_ref, sent_ref, panel_ref = rest[count:]
    rank = ranks_ref.shape[0] // 2
    for k in range(count):
        panel_ref[pl.ds(k * rank, rank), :] = ups[k][...]
    contract = (((0,), (0,)), ((), ()))
    summed = ranks_ref[...] + got_ref[...]
    for i, homes in enumerate((homes_ref, other_homes_ref)):
        shrunk = summed[i * rank : (i + 1) * rank]
        spread = jnp.concatenate([jnp.where(homes[...] == ids_ref[1 + k], shrunk, 0.0) for k in range(count)], axis=0)
        delta = lax.dot_general(spread.astype(jnp.bfloat16), panel_ref[...], contract, preferred_element_type=jnp.float32)
        if i == 0:
            own_ref[...] = delta + (kept_ref[...] + base_ref[...])
        else:
            sent_ref[...] = delta.astype(sent_ref.dtype)


def gathered_values(rows, down, up, homes, base_kept, base_sent):
    slots, features = rows.shape
    rank, columns = up.shape
    replicas = lax.axis_size("replica")
    half = rank // 2
    outer, inner = lax.axis_index("replica") // 2, lax.axis_index("replica") % 2
    start = lax.axis_index("group") * half
    held = [(0, lax.dynamic_slice_in_dim(down, start, half, 0), up)]
    bit = replicas // 4
    while bit:
        came = [(offset ^ bit, swap(part, "replica", 2 * bit), swap(raised, "replica", 2 * bit)) for offset, part, raised in held]
        if len(held) == 1:
            offset, *parts = came[0]
            parts, base_sent = lax.optimization_barrier((parts, base_sent))
            came = [(offset, *parts)]
        held = held + came
        bit //= 2
    base_got = swap(base_sent, "tensor", 1)
    offsets = [offset for offset, _, _ in held]
    mine = [part for _, part, _ in held[1:]]
    theirs = [swap(part, "group", 1) for part in mine]
    ups = [raised for _, _, raised in held]
    other_rows = swap(rows, "replica", 1)
    homes = homes[None, :]
    other_homes = swap(homes, "replica", 1)
    ids = jnp.stack([start] + [(outer ^ offset) * 2 + inner for offset in offsets]).astype(jnp.int32)
    vmem = pl.BlockSpec(memory_space=pltpu.VMEM)
    smem = pl.BlockSpec(memory_space=pltpu.SMEM)
    inputs = [rows, other_rows, homes, other_homes, down] + mine + theirs
    ranks = pl.pallas_call(
        functools.partial(rank_kernel, offsets, half),
        in_specs=[smem] + [vmem] * len(inputs),
        out_specs=vmem,
        out_shape=jax.ShapeDtypeStruct((2 * rank, slots), jnp.float32),
        scratch_shapes=[pltpu.VMEM((len(offsets) * rank, features), jnp.bfloat16)],
        compiler_params=pltpu.CompilerParams(vmem_limit_bytes=16 << 20),
    )(ids, *inputs)
    inputs = [homes, other_homes, ranks, swap(ranks, "tensor", 1), base_kept, base_got] + ups
    own, sent = pl.pallas_call(
        functools.partial(delta_kernel, len(ups)),
        in_specs=[smem] + [vmem] * len(inputs),
        out_specs=[vmem, vmem],
        out_shape=[
            jax.ShapeDtypeStruct((slots, columns), jnp.float32),
            jax.ShapeDtypeStruct((slots, columns), jnp.bfloat16),
        ],
        scratch_shapes=[pltpu.VMEM((len(ups) * rank, columns), jnp.bfloat16)],
        compiler_params=pltpu.CompilerParams(vmem_limit_bytes=16 << 20),
    )(ids, *inputs)
    return own, swap(sent, "replica", 1)


def local(
    hidden,
    queries,
    incoming_keys,
    stored_key_cache,
    stored_value_cache,
    base_value_weight,
    adapter_down_rows,
    adapter_up_rows,
    request_adapter,
    adapter_replica,
    replica_slot_count,
    cache_length,
):
    slots, _, features = hidden.shape
    heads, _, size = stored_key_cache.shape[1:]
    query_heads = queries.shape[3] // size
    replicas = lax.axis_size("replica")
    matches = request_adapter[:, None] == jnp.arange(adapter_replica.shape[0], dtype=jnp.int32)[None, :]
    homes = jnp.sum(jnp.where(matches, adapter_replica[None, :], 0), axis=1)
    rows = hidden.reshape(slots, features)
    down, up = adapter_down_rows[0], adapter_up_rows[0]
    query_rows = queries.reshape(slots, heads, query_heads, size).transpose(0, 2, 1, 3).reshape(-1, size)
    scalars = jnp.stack([replica_slot_count[0], lax.axis_index("tensor")]).astype(jnp.int32)
    base_kept, base_sent, mixed, share = base_and_cached(
        rows, base_value_weight, query_rows, incoming_keys, stored_key_cache, stored_value_cache, cache_length, scalars
    )
    power = replicas >= 4 and replicas & (replicas - 1) == 0
    if power and lax.axis_size("group") == 2 and replicas * down.size <= GATHER_BYTES:
        own, returned = gathered_values(rows, down, up, homes, base_kept, base_sent)
    else:
        live_mask = jnp.arange(slots, dtype=jnp.int32) < replica_slot_count[0]
        own, returned = base_kept + swap(base_sent, "tensor", 1), moved_delta(rows, down, up, homes, live_mask)
    attention, fresh_values = finish(own, returned, mixed, share, replica_slot_count)
    attention = attention.reshape(slots, query_heads, heads, size).transpose(0, 2, 1, 3)
    return (
        attention.reshape(slots, 1, heads, query_heads * size),
        fresh_values.reshape(slots, 1, heads, size),
    )


def solution(mesh):
    placed = (
        P(("group", "replica"), None, "tensor"),
        P(("group", "replica"), None, "tensor", None),
        P(("group", "replica"), None, "tensor", None),
        P(("group", "replica"), "tensor", None, None),
        P(("group", "replica"), "tensor", None, None),
        P("tensor", None),
        P("replica", None, "tensor"),
        P("replica", None, "tensor"),
        P("replica"),
        P(),
        P("replica"),
        P("replica"),
    )
    return jax.shard_map(
        local,
        mesh=mesh,
        in_specs=placed,
        out_specs=(
            P(("group", "replica"), None, "tensor", None),
            P(("group", "replica"), None, "tensor", None),
        ),
        check_vma=False,
    )
```

time: 70.1 us -> 40.9 us (0.58)
  between operations: 15 us -> 1.39 us
  Pallas kernels: 0 us -> 9.56 us
  waiting for transfers between devices: 20.8 us -> 11.8 us
  matrix products: 8.28 us -> 0 us
  starting transfers between devices: 10.8 us -> 15.3 us
  other arithmetic: 4.9 us -> 0.68 us
  local copies, waits for them, and re-layouts: 5.96 us -> 1.93 us
  blocking collectives: 3.69 us -> 0 us
    all_to_all x2 -> x0, waiting for transfers between devices: 20.8 us -> none  [the longest x1 14.3 us: local(): lax.all_to_all(outgoing, 'replica', split_axis=0, concat_axis=0, tiled=True)]
    ppermute x0 -> x14, starting transfers between devices: none -> 15.3 us  [swap(): return lax.ppermute(array, axis, [(i, i ^ bit) for i in range(size)])]
    ppermute x0 -> x14, waiting for transfers between devices: none -> 11.8 us  [swap(): return lax.ppermute(array, axis, [(i, i ^ bit) for i in range(size)])]
    all_to_all x2 -> x0, starting transfers between devices: 10.8 us -> none  [the longest x1 7.25 us: local(): lax.all_to_all(outgoing, 'replica', split_axis=0, concat_axis=0, tiled=True)]
    pallas_call x0 -> x4, Pallas kernels: none -> 9.56 us  [the longest x1 6.51 us: base_and_cached(): pl.pallas_call(functools.partial(cached_kernel, dims), grid_spec=pltpu.Pr...]
    dot_general x6 -> x0, matrix products: 8.28 us -> none  [the longest x1 2.59 us: attend(): jnp.einsum('rsghd,rgpd->rsghp', grouped, cached_keys, preferred_element_t...]
    psum x1 -> x0, blocking collectives: 3.69 us -> none  [local(): summed_rank = lax.psum(partial_rank, 'tensor')]
    scatter x1 -> x0, local copies, waits for them, and re-layouts: 2.61 us -> none  [local(): outgoing = outgoing.at[target].set(hidden, mode='drop').reshape(replicas,...]
  transfers between devices with their start and end apart: 3 -> 14, of which waited for: 2 -> 5; matrix products, arithmetic and copies ran while one was open for 15% -> 2% of each run, Pallas kernels for 0% -> 19%
where the time goes in v1:
time: 40.9 us; the launch traced here: 40.7 us
  starting transfers between devices  15.3 us (37%)
  waiting for transfers between devices  11.8 us (29%)
  Pallas kernels  9.56 us (23%)
  local copies, waits for them, and re-layouts  1.93 us (5%)
  between operations  1.39 us (3%)
  other arithmetic  0.68 us (2%)
    ppermute x14, starting transfers between devices, swap(): return lax.ppermute(array, axis, [(i, i ^ bit) for i in range(size)])  15.3 us
    ppermute x14, waiting for transfers between devices, swap(): return lax.ppermute(array, axis, [(i, i ^ bit) for i in range(size)])  11.8 us
    pallas_call x1, Pallas kernels, base_and_cached(): pl.pallas_call(functools.partial(cached_kernel, dims), grid_spec=pltpu.Pr...  6.51 us
    pallas_call x1, Pallas kernels, gathered_values(): pl.pallas_call(functools.partial(rank_kernel, offsets, half), in_specs=[s...  1.28 us
    pallas_call x1, Pallas kernels, finish(): pl.pallas_call(final_kernel, in_specs=[pl.BlockSpec(memory_space=pltpu.SM...  1 us
    unnamed x16, local copies, waits for them, and re-layouts  0.92 us
    dynamic_slice x1, local copies, waits for them, and re-layouts, gathered_values(): held = [(0, lax.dynamic_slice_in_dim(down, start, half, 0), up)]  0.92 us
  transfers between devices with their start and end apart: 14, of which 5 were waited for; matrix products, arithmetic and copies ran while one was open for 2% of the time, Pallas kernels for 19%

profile of v1, /device:TPU:0, one launch (start us, length us, event | category | flops | bytes accessed | tf_op | source)
XLA Modules:
  0.0 40.7 jit_solution(8257016346656631141)
XLA Ops:
  0.6 0.9 %dynamic-slice_bitcast_fusion = bf16[32,2048]{1,0:T(8,128)(2,1)S(1)} fusion(bf16[1,64,2048]{2,1,0:T(8,128)(2,1)} %param.18, s32[]{:T(128)S(6)} %select_n.21), kind=kLoop, calls=%fused_computation | loop fusion | bytes 262148 | tf_op jit(solution)/shard_map/dynamic_slice | solution.py:237
  1.6 4.1 %collective-permute-start.2 = (bf16[32,2048]{1,0:T(8,128)(2,1)S(1)}, bf16[32,2048]{1,0:T(8,128)(2,1)S(1)}, u32[]{:S(2)}, u32[]{:S(2)}) collective-permute-start(bf16[32,2048]{1,0:T(8,128)(2,1)S(1)} %dynamic-slice_bitcast_fusion), channel_id=1, source_target_pairs={{0,8},{2,10},{4,12},{6,14},{8,0},{10,2},{12,4},{14,6},{1,9},{3,11}... | collective-permute-start | bytes 393224 | tf_op jit(solution)/shard_map/ppermute | solution.py:17
  5.7 1.6 %collective-permute-start.4 = (bf16[32,2048]{1,0:T(8,128)(2,1)S(1)}, bf16[32,2048]{1,0:T(8,128)(2,1)S(1)}, u32[]{:S(2)}, u32[]{:S(2)}) collective-permute-start(bf16[32,2048]{1,0:T(8,128)(2,1)S(1)} %dynamic-slice_bitcast_fusion), channel_id=1, source_target_pairs={{0,4},{2,6},{4,0},{6,2},{8,12},{10,14},{12,8},{14,10},{1,5},{3,7},... | collective-permute-start | bytes 393224 | tf_op jit(solution)/shard_map/ppermute | solution.py:17
  7.2 0.3 collective-permute-start.3
  7.6 1.5 %collective-permute-start.1 = (bf16[96,2048]{1,0:T(8,128)(2,1)}, bf16[96,2048]{1,0:T(8,128)(2,1)S(1)}, u32[]{:S(2)}, u32[]{:S(2)}) collective-permute-start(bf16[96,2048]{1,0:T(8,128)(2,1)} %bitcast.28), channel_id=1, source_target_pairs={{0,2},{2,0},{4,6},{6,4},{8,10},{10,8},{12,14},{14,12},{1,3},{3,1},... | collective-permute-start | bytes 1179656 | tf_op jit(solution)/shard_map/ppermute | solution.py:17
  9.7 0.6 %pad_add_fusion.scalars_ref = s32[2]{0:T(128)} fusion(s32[1]{0:T(128)} %bitcast.10, s32[1]{0:T(128)S(6)} %copy.20.count_ref), kind=kLoop, calls=%fused_computation.3 | loop fusion | flops 2 | bytes 16 | tf_op jit(solution)/shard_map/stack | solution.py:305
  10.3 0.0 copy-start.6
  10.3 0.0 copy-start.7
  10.3 0.0 copy-start
  10.3 0.0 copy-start.2
  10.3 0.0 copy-start.5
  10.3 6.5 %shard_map.131 = (f32[96,256]{1,0:T(8,128)}, f32[96,256]{1,0:T(8,128)}, f32[1536,128]{1,0:T(8,128)}, bf16[1536,48]{1,0:T(8,128)(2,1)}) custom-call(s32[96]{0:T(128)} %lengths_ref.1, s32[2]{0:T(128)} %pad_add_fusion.scalars_ref, bf16[96,2048]{1,0:T(8,128)(2,1)} %bitcast.29, bf16[2048,512]{1,0:T(8,128)(2,1)} %weight_ref.1, bf16[1536,128]{1,0:T(8,128)(2,1)} %bitcast.40, ...), custom_call_target="tpu_custom_call" | custom-call | flops 268435456 | bytes 12582912 | tf_op jit(solution)/shard_map/pallas_call | solution.py:96
  16.8 0.0 copy-start.1
  16.8 0.0 copy-start.3
  16.9 0.0 collective-permute-done.3.rest_1_
  16.9 0.0 collective-permute-done.2.rest_0_
  16.9 0.5 %collective-permute-start.5 = (bf16[32,2048]{1,0:T(8,128)(2,1)S(1)}, bf16[32,2048]{1,0:T(8,128)(2,1)S(1)}, u32[]{:S(2)}, u32[]{:S(2)}) collective-permute-start(bf16[32,2048]{1,0:T(8,128)(2,1)S(1)} %collective-permute-done.2.rest_0_), channel_id=1, source_target_pairs={{0,4},{2,6},{4,0},{6,2},{8,12},{10,14},{12,8},{14,10},{1,5},{3,7},... | collective-permute-start | bytes 393224 | tf_op jit(solution)/shard_map/ppermute | solution.py:17
  17.4 1.5 %collective-permute-start.6 = (bf16[32,2048]{1,0:T(8,128)(2,1)S(1)}, bf16[32,2048]{1,0:T(8,128)(2,1)S(1)}, u32[]{:S(2)}, u32[]{:S(2)}) collective-permute-start(bf16[32,2048]{1,0:T(8,128)(2,1)S(1)} %collective-permute-done.2.rest_0_), channel_id=1, source_target_pairs={{0,16},{16,0},{1,17},{17,1},{2,18},{18,2},{3,19},{19,3},{4,20},{20... | collective-permute-start | bytes 393224 | tf_op jit(solution)/shard_map/ppermute | solution.py:17
  18.9 0.0 collective-permute-done.4.rest_1_
  18.9 0.5 %collective-permute-start.7 = (bf16[32,2048]{1,0:T(8,128)(2,1)S(1)}, bf16[32,2048]{1,0:T(8,128)(2,1)S(1)}, u32[]{:S(2)}, u32[]{:S(2)}) collective-permute-start(bf16[32,2048]{1,0:T(8,128)(2,1)S(1)} %collective-permute-done.4.rest_1_), channel_id=1, source_target_pairs={{0,16},{16,0},{1,17},{17,1},{2,18},{18,2},{3,19},{19,3},{4,20},{20... | collective-permute-start | bytes 393224 | tf_op jit(solution)/shard_map/ppermute | solution.py:17
  19.4 2.5 %collective-permute-done.5.rest_2_ = bf16[32,2048]{1,0:T(8,128)(2,1)S(1)} collective-permute-done((bf16[32,2048]{1,0:T(8,128)(2,1)S(1)}, bf16[32,2048]{1,0:T(8,128)(2,1)S(1)}, u32[]{:S(2)}, u32[]{:S(2)}) %collective-permute-start.5) | collective-permute-done | bytes 131104 | tf_op jit(solution)/shard_map/ppermute | solution.py:17
  21.9 1.5 %collective-permute-start.8 = (bf16[32,2048]{1,0:T(8,128)(2,1)S(1)}, bf16[32,2048]{1,0:T(8,128)(2,1)S(1)}, u32[]{:S(2)}, u32[]{:S(2)}) collective-permute-start(bf16[32,2048]{1,0:T(8,128)(2,1)S(1)} %collective-permute-done.5.rest_2_), channel_id=1, source_target_pairs={{0,16},{16,0},{1,17},{17,1},{2,18},{18,2},{3,19},{19,3},{4,20},{20... | collective-permute-start | bytes 393224 | tf_op jit(solution)/shard_map/ppermute | solution.py:17
  23.4 0.0 copy-done.6
  23.4 0.0 copy-done.7
  23.4 0.1 select_reduce_fusion
  23.5 0.5 %collective-permute-start = (s32[1,96]{1,0:T(1,128)S(1)}, s32[1,96]{1,0:T(1,128)S(1)}, u32[]{:S(2)}, u32[]{:S(2)}) collective-permute-start(s32[1,96]{1,0:T(1,128)S(1)} %bitcast.35), channel_id=1, source_target_pairs={{0,2},{2,0},{4,6},{6,4},{8,10},{10,8},{12,14},{14,12},{1,3},{3,1},... | collective-permute-start | bytes 1160 | tf_op jit(solution)/shard_map/ppermute | solution.py:17
  24.1 3.0 %collective-permute-done.other_homes_ref = s32[1,96]{1,0:T(1,128)S(1)} collective-permute-done((s32[1,96]{1,0:T(1,128)S(1)}, s32[1,96]{1,0:T(1,128)S(1)}, u32[]{:S(2)}, u32[]{:S(2)}) %collective-permute-start) | collective-permute-done | bytes 416 | tf_op jit(solution)/shard_map/ppermute | solution.py:17
  27.1 0.0 collective-permute-start.10
  27.1 0.1 stack.29.ids_ref
  27.2 0.0 collective-permute-done.6.rest_3_
  27.2 0.0 collective-permute-done.7.rest_4_
  27.2 0.0 collective-permute-done.8.rest_5_
  27.2 0.0 collective-permute-done.1.other_ref
  27.2 0.0 copy-done
  27.2 0.0 copy-done.2
  27.2 1.3 %shard_map.132.ranks_ref = f32[128,96]{1,0:T(8,128)S(1)} custom-call(s32[5]{0:T(128)S(1)} %stack.29.ids_ref, bf16[96,2048]{1,0:T(8,128)(2,1)S(1)} %bitcast.30, bf16[96,2048]{1,0:T(8,128)(2,1)S(1)} %collective-permute-done.1.other_ref, s32[1,96]{1,0:T(1,128)S(1)} %bitcast.36, s32[1,96]{1,0:T(1,128)S(1)} %collective-permute-done.other_homes_ref, ...), custom_call_target="tpu_custom_call" | custom-call | tf_op jit(solution)/shard_map/pallas_call | solution.py:259
  28.5 0.6 %collective-permute-start.9 = (f32[128,96]{1,0:T(8,128)S(1)}, f32[128,96]{1,0:T(8,128)S(1)}, u32[]{:S(2)}, u32[]{:S(2)}) collective-permute-start(f32[128,96]{1,0:T(8,128)S(1)} %shard_map.132.ranks_ref), channel_id=1, source_target_pairs={{0,1},{1,0},{2,3},{3,2},{4,5},{5,4},{6,7},{7,6},{8,9},{9,8},{10,11... | collective-permute-start | bytes 147464 | tf_op jit(solution)/shard_map/ppermute | solution.py:17
  29.1 0.0 copy-done.5
  29.1 0.9 %collective-permute-start.11 = (bf16[64,256]{1,0:T(8,128)(2,1)S(1)}, bf16[64,256]{1,0:T(8,128)(2,1)S(1)}, u32[]{:S(2)}, u32[]{:S(2)}) collective-permute-start(bf16[64,256]{1,0:T(8,128)(2,1)S(1)} %bitcast.33), channel_id=1, source_target_pairs={{0,4},{2,6},{4,0},{6,2},{8,12},{10,14},{12,8},{14,10},{1,5},{3,7},... | collective-permute-start | bytes 98312 | tf_op jit(solution)/shard_map/ppermute | solution.py:17
  29.9 1.2 %collective-permute-start.12 = (bf16[64,256]{1,0:T(8,128)(2,1)S(1)}, bf16[64,256]{1,0:T(8,128)(2,1)S(1)}, u32[]{:S(2)}, u32[]{:S(2)}) collective-permute-start(bf16[64,256]{1,0:T(8,128)(2,1)S(1)} %collective-permute-done.3.rest_1_), channel_id=1, source_target_pairs={{0,4},{2,6},{4,0},{6,2},{8,12},{10,14},{12,8},{14,10},{1,5},{3,7},... | collective-permute-start | bytes 98312 | tf_op jit(solution)/shard_map/ppermute | solution.py:17
  31.1 2.2 %collective-permute-done.11.rest_2_ = bf16[64,256]{1,0:T(8,128)(2,1)S(1)} collective-permute-done((bf16[64,256]{1,0:T(8,128)(2,1)S(1)}, bf16[64,256]{1,0:T(8,128)(2,1)S(1)}, u32[]{:S(2)}, u32[]{:S(2)}) %collective-permute-start.11) | collective-permute-done | bytes 32800 | tf_op jit(solution)/shard_map/ppermute | solution.py:17
  33.3 0.5 %collective-permute-done.12.rest_3_ = bf16[64,256]{1,0:T(8,128)(2,1)S(1)} collective-permute-done((bf16[64,256]{1,0:T(8,128)(2,1)S(1)}, bf16[64,256]{1,0:T(8,128)(2,1)S(1)}, u32[]{:S(2)}, u32[]{:S(2)}) %collective-permute-start.12) | collective-permute-done | bytes 32800 | tf_op jit(solution)/shard_map/ppermute | solution.py:17
  33.8 0.0 collective-permute-done.10.base_ref
  33.8 0.0 collective-permute-done.9.got_ref
  33.8 0.0 copy-start.4
  33.8 0.9 %copy-done.4 = f32[96,256]{1,0:T(8,128)S(1)} copy-done((f32[96,256]{1,0:T(8,128)S(1)}, f32[96,256]{1,0:T(8,128)}, u32[]{:S(2)}) %copy-start.4) | copy-done | bytes 98328
  34.7 0.8 %shard_map.133 = (f32[96,256]{1,0:T(8,128)S(1)}, bf16[96,256]{1,0:T(8,128)(2,1)S(1)}) custom-call(s32[5]{0:T(128)S(1)} %stack.29.ids_ref, s32[1,96]{1,0:T(1,128)S(1)} %bitcast.37, s32[1,96]{1,0:T(1,128)S(1)} %collective-permute-done.other_homes_ref, f32[128,96]{1,0:T(8,128)S(1)} %shard_map.132.ranks_ref, f32[128,96]{1,0:T(8,128)S(1)} %collective-permute-done.9.got_ref, ...), custom_call_target="tpu_custom_call" | custom-call | tf_op jit(solution)/shard_map/pallas_call | solution.py:268
  35.5 0.6 %collective-permute-start.13 = (bf16[96,256]{1,0:T(8,128)(2,1)S(1)}, bf16[96,256]{1,0:T(8,128)(2,1)S(1)}, u32[]{:S(2)}, u32[]{:S(2)}) collective-permute-start(bf16[96,256]{1,0:T(8,128)(2,1)S(1)} %get-tuple-element.19), channel_id=1, source_target_pairs={{0,2},{2,0},{4,6},{6,4},{8,10},{10,8},{12,14},{14,12},{1,3},{3,1},... | collective-permute-start | bytes 147464 | tf_op jit(solution)/shard_map/ppermute | solution.py:17
  36.1 3.6 %collective-permute-done.13.returned_ref = bf16[96,256]{1,0:T(8,128)(2,1)S(1)} collective-permute-done((bf16[96,256]{1,0:T(8,128)(2,1)S(1)}, bf16[96,256]{1,0:T(8,128)(2,1)S(1)}, u32[]{:S(2)}, u32[]{:S(2)}) %collective-permute-start.13) | collective-permute-done | bytes 49184 | tf_op jit(solution)/shard_map/ppermute | solution.py:17
  39.7 0.0 copy-done.1
  39.7 0.0 copy-done.3
  39.7 1.0 %shard_map.134 = (bf16[1536,128]{1,0:T(8,128)(2,1)}, bf16[192,128]{1,0:T(8,128)(2,1)}) custom-call(s32[1]{0:T(128)S(6)} %copy.20.count_ref, f32[96,256]{1,0:T(8,128)S(1)} %get-tuple-element.18.own_ref, bf16[96,256]{1,0:T(8,128)(2,1)S(1)} %collective-permute-done.13.returned_ref, f32[1536,128]{1,0:T(8,128)S(1)} %copy-done.1, bf16[1536,48]{1,0:T(8,128)(2,1)S(1)} %copy-done.3), custom_call_target="tpu_custom_call" | custom-call | tf_op jit(solution)/shard_map/pallas_call | solution.py:162
Async XLA Ops:
  1.6 15.3 %collective-permute-start.2 = (bf16[32,2048]{1,0:T(8,128)(2,1)S(1)}, bf16[32,2048]{1,0:T(8,128)(2,1)S(1)}, u32[]{:S(2)}, u32[]{:S(2)}) collective-permute-start(bf16[32,2048]{1,0:T(8,128)(2,1)S(1)} %dynamic-slice_bitcast_fusion), channel_id=1, source_target_pairs={{0,8},{2,10},{4,12},{6,14},{8,0},{10,2},{12,4},{14,6},{1,9},{3,11}... | collective-permute-start | bytes 393224 | tf_op jit(solution)/shard_map/ppermute | solution.py:17
  5.7 13.3 %collective-permute-start.4 = (bf16[32,2048]{1,0:T(8,128)(2,1)S(1)}, bf16[32,2048]{1,0:T(8,128)(2,1)S(1)}, u32[]{:S(2)}, u32[]{:S(2)}) collective-permute-start(bf16[32,2048]{1,0:T(8,128)(2,1)S(1)} %dynamic-slice_bitcast_fusion), channel_id=1, source_target_pairs={{0,4},{2,6},{4,0},{6,2},{8,12},{10,14},{12,8},{14,10},{1,5},{3,7},... | collective-permute-start | bytes 393224 | tf_op jit(solution)/shard_map/ppermute | solution.py:17
  7.2 9.6 %collective-permute-start.3 = (bf16[64,256]{1,0:T(8,128)(2,1)}, bf16[64,256]{1,0:T(8,128)(2,1)S(1)}, u32[]{:S(2)}, u32[]{:S(2)}) collective-permute-start(bf16[64,256]{1,0:T(8,128)(2,1)} %bitcast.32), channel_id=1, source_target_pairs={{0,8},{2,10},{4,12},{6,14},{8,0},{10,2},{12,4},{14,6},{1,9},{3,11}... | collective-permute-start | bytes 98312 | tf_op jit(solution)/shard_map/ppermute | solution.py:17
  7.6 19.6 %collective-permute-start.1 = (bf16[96,2048]{1,0:T(8,128)(2,1)}, bf16[96,2048]{1,0:T(8,128)(2,1)S(1)}, u32[]{:S(2)}, u32[]{:S(2)}) collective-permute-start(bf16[96,2048]{1,0:T(8,128)(2,1)} %bitcast.28), channel_id=1, source_target_pairs={{0,2},{2,0},{4,6},{6,4},{8,10},{10,8},{12,14},{14,12},{1,3},{3,1},... | collective-permute-start | bytes 1179656 | tf_op jit(solution)/shard_map/ppermute | solution.py:17
  10.3 13.1 %copy-start.6 = (s32[8]{0:T(128)S(1)}, s32[8]{0:T(128)}, u32[]{:S(2)}) copy-start(s32[8]{0:T(128)} %param.21) | copy-start | bytes 100
  10.3 13.1 %copy-start.7 = (s32[96]{0:T(128)S(1)}, s32[96]{0:T(128)}, u32[]{:S(2)}) copy-start(s32[96]{0:T(128)} %param.20) | copy-start | bytes 1156
  10.3 16.9 %copy-start = (bf16[96,1,2048]{2,0,1:T(8,128)(2,1)S(1)}, bf16[96,1,2048]{2,0,1:T(8,128)(2,1)}, u32[]{:S(2)}) copy-start(bf16[96,1,2048]{2,0,1:T(8,128)(2,1)} %param.12) | copy-start | bytes 1179652
  10.3 16.9 %copy-start.2 = (bf16[1,64,2048]{2,1,0:T(8,128)(2,1)S(1)}, bf16[1,64,2048]{2,1,0:T(8,128)(2,1)}, u32[]{:S(2)}) copy-start(bf16[1,64,2048]{2,1,0:T(8,128)(2,1)} %param.18) | copy-start | bytes 786436
  10.3 18.7 %copy-start.5 = (bf16[1,64,256]{2,1,0:T(8,128)(2,1)S(1)}, bf16[1,64,256]{2,1,0:T(8,128)(2,1)}, u32[]{:S(2)}) copy-start(bf16[1,64,256]{2,1,0:T(8,128)(2,1)} %param.19) | copy-start | bytes 98308
  16.8 22.8 %copy-start.1 = (f32[1536,128]{1,0:T(8,128)S(1)}, f32[1536,128]{1,0:T(8,128)}, u32[]{:S(2)}) copy-start(f32[1536,128]{1,0:T(8,128)} %get-tuple-element.20.mixed_ref) | copy-start | bytes 2359300
  16.8 22.8 %copy-start.3 = (bf16[1536,48]{1,0:T(8,128)(2,1)S(1)}, bf16[1536,48]{1,0:T(8,128)(2,1)}, u32[]{:S(2)}) copy-start(bf16[1536,48]{1,0:T(8,128)(2,1)} %get-tuple-element.21.share_ref) | copy-start | bytes 442372
  16.9 5.0 %collective-permute-start.5 = (bf16[32,2048]{1,0:T(8,128)(2,1)S(1)}, bf16[32,2048]{1,0:T(8,128)(2,1)S(1)}, u32[]{:S(2)}, u32[]{:S(2)}) collective-permute-start(bf16[32,2048]{1,0:T(8,128)(2,1)S(1)} %collective-permute-done.2.rest_0_), channel_id=1, source_target_pairs={{0,4},{2,6},{4,0},{6,2},{8,12},{10,14},{12,8},{14,10},{1,5},{3,7},... | collective-permute-start | bytes 393224 | tf_op jit(solution)/shard_map/ppermute | solution.py:17
  17.4 9.8 %collective-permute-start.6 = (bf16[32,2048]{1,0:T(8,128)(2,1)S(1)}, bf16[32,2048]{1,0:T(8,128)(2,1)S(1)}, u32[]{:S(2)}, u32[]{:S(2)}) collective-permute-start(bf16[32,2048]{1,0:T(8,128)(2,1)S(1)} %collective-permute-done.2.rest_0_), channel_id=1, source_target_pairs={{0,16},{16,0},{1,17},{17,1},{2,18},{18,2},{3,19},{19,3},{4,20},{20... | collective-permute-start | bytes 393224 | tf_op jit(solution)/shard_map/ppermute | solution.py:17
  18.9 8.2 %collective-permute-start.7 = (bf16[32,2048]{1,0:T(8,128)(2,1)S(1)}, bf16[32,2048]{1,0:T(8,128)(2,1)S(1)}, u32[]{:S(2)}, u32[]{:S(2)}) collective-permute-start(bf16[32,2048]{1,0:T(8,128)(2,1)S(1)} %collective-permute-done.4.rest_1_), channel_id=1, source_target_pairs={{0,16},{16,0},{1,17},{17,1},{2,18},{18,2},{3,19},{19,3},{4,20},{20... | collective-permute-start | bytes 393224 | tf_op jit(solution)/shard_map/ppermute | solution.py:17
  21.9 5.2 %collective-permute-start.8 = (bf16[32,2048]{1,0:T(8,128)(2,1)S(1)}, bf16[32,2048]{1,0:T(8,128)(2,1)S(1)}, u32[]{:S(2)}, u32[]{:S(2)}) collective-permute-start(bf16[32,2048]{1,0:T(8,128)(2,1)S(1)} %collective-permute-done.5.rest_2_), channel_id=1, source_target_pairs={{0,16},{16,0},{1,17},{17,1},{2,18},{18,2},{3,19},{19,3},{4,20},{20... | collective-permute-start | bytes 393224 | tf_op jit(solution)/shard_map/ppermute | solution.py:17
  23.5 3.5 %collective-permute-start = (s32[1,96]{1,0:T(1,128)S(1)}, s32[1,96]{1,0:T(1,128)S(1)}, u32[]{:S(2)}, u32[]{:S(2)}) collective-permute-start(s32[1,96]{1,0:T(1,128)S(1)} %bitcast.35), channel_id=1, source_target_pairs={{0,2},{2,0},{4,6},{6,4},{8,10},{10,8},{12,14},{14,12},{1,3},{3,1},... | collective-permute-start | bytes 1160 | tf_op jit(solution)/shard_map/ppermute | solution.py:17
  27.1 6.8 %collective-permute-start.10 = (f32[96,256]{1,0:T(8,128)}, f32[96,256]{1,0:T(8,128)S(1)}, u32[]{:S(2)}, u32[]{:S(2)}) collective-permute-start(f32[96,256]{1,0:T(8,128)} %get-tuple-element.16), channel_id=1, source_target_pairs={{0,1},{1,0},{2,3},{3,2},{4,5},{5,4},{6,7},{7,6},{8,9},{9,8},{10,11... | collective-permute-start | bytes 294920 | tf_op jit(solution)/shard_map/ppermute | solution.py:17
  28.5 5.3 %collective-permute-start.9 = (f32[128,96]{1,0:T(8,128)S(1)}, f32[128,96]{1,0:T(8,128)S(1)}, u32[]{:S(2)}, u32[]{:S(2)}) collective-permute-start(f32[128,96]{1,0:T(8,128)S(1)} %shard_map.132.ranks_ref), channel_id=1, source_target_pairs={{0,1},{1,0},{2,3},{3,2},{4,5},{5,4},{6,7},{7,6},{8,9},{9,8},{10,11... | collective-permute-start | bytes 147464 | tf_op jit(solution)/shard_map/ppermute | solution.py:17
  29.1 4.2 %collective-permute-start.11 = (bf16[64,256]{1,0:T(8,128)(2,1)S(1)}, bf16[64,256]{1,0:T(8,128)(2,1)S(1)}, u32[]{:S(2)}, u32[]{:S(2)}) collective-permute-start(bf16[64,256]{1,0:T(8,128)(2,1)S(1)} %bitcast.33), channel_id=1, source_target_pairs={{0,4},{2,6},{4,0},{6,2},{8,12},{10,14},{12,8},{14,10},{1,5},{3,7},... | collective-permute-start | bytes 98312 | tf_op jit(solution)/shard_map/ppermute | solution.py:17
  29.9 3.9 %collective-permute-start.12 = (bf16[64,256]{1,0:T(8,128)(2,1)S(1)}, bf16[64,256]{1,0:T(8,128)(2,1)S(1)}, u32[]{:S(2)}, u32[]{:S(2)}) collective-permute-start(bf16[64,256]{1,0:T(8,128)(2,1)S(1)} %collective-permute-done.3.rest_1_), channel_id=1, source_target_pairs={{0,4},{2,6},{4,0},{6,2},{8,12},{10,14},{12,8},{14,10},{1,5},{3,7},... | collective-permute-start | bytes 98312 | tf_op jit(solution)/shard_map/ppermute | solution.py:17
  33.8 0.9 %copy-start.4 = (f32[96,256]{1,0:T(8,128)S(1)}, f32[96,256]{1,0:T(8,128)}, u32[]{:S(2)}) copy-start(f32[96,256]{1,0:T(8,128)} %get-tuple-element.15.kept_ref) | copy-start | bytes 294916
  35.5 4.2 %collective-permute-start.13 = (bf16[96,256]{1,0:T(8,128)(2,1)S(1)}, bf16[96,256]{1,0:T(8,128)(2,1)S(1)}, u32[]{:S(2)}, u32[]{:S(2)}) collective-permute-start(bf16[96,256]{1,0:T(8,128)(2,1)S(1)} %get-tuple-element.19), channel_id=1, source_target_pairs={{0,2},{2,0},{4,6},{6,4},{8,10},{10,8},{12,14},{14,12},{1,3},{3,1},... | collective-permute-start | bytes 147464 | tf_op jit(solution)/shard_map/ppermute | solution.py:17

commit v2 on v1

v2 whole, which is shorter than its diff:
```python
import functools
import math

import jax
import jax.numpy as jnp
from jax import lax
from jax.experimental import pallas as pl
from jax.experimental.pallas import tpu as pltpu
from jax.sharding import PartitionSpec as P

NEGATIVE = -1e30
GATHER_BYTES = 1 << 22


def swap(array, axis, bit):
    size = lax.axis_size(axis)
    return lax.ppermute(array, axis, [(i, i ^ bit) for i in range(size)])


def cached_kernel(dims, lengths_ref, count_ref, *refs):
    heads, query_heads, context, group, parts, scale = dims
    sources, outputs, buffers, results = refs[:4], refs[4:6], refs[6:10], refs[10:12]
    in_sems, out_sems = refs[12:]

    def copy_of(source, target, sem, part):
        size = source.shape[0] // parts
        at = pl.ds(part * size, size)
        return pltpu.make_async_copy(source.at[at], target.at[at], sem)

    copies = [
        [copy_of(source, buffer, in_sems.at[part, i], part) for i, (source, buffer) in enumerate(zip(sources, buffers))]
        for part in range(parts)
    ]
    writes = [
        [copy_of(result, output, out_sems.at[part, i], part) for i, (result, output) in enumerate(zip(results, outputs))]
        for part in range(parts)
    ]
    for group_of_copies in copies:
        for copy in group_of_copies:
            copy.start()
    query_ref, key_ref, fresh_ref, value_ref = buffers
    mixed_ref, share_ref = results

    slots = group // heads
    rows, places = group * query_heads, group * context
    part_rows = query_ref.shape[0] // parts
    part_pairs = fresh_ref.shape[0] // parts
    blocks = part_rows // rows
    contract = (((1,), (1,)), ((), ()))

    def pair_of(shape):
        row = lax.broadcasted_iota(jnp.int32, shape, 0)
        return row // (heads * query_heads) * heads + row % heads

    own = pair_of((rows, places)) == lax.broadcasted_iota(jnp.int32, (rows, places), 1) // context
    own_fresh = pair_of((part_rows, part_pairs)) == lax.broadcasted_iota(jnp.int32, (part_rows, part_pairs), 1)
    row_slot = lax.broadcasted_iota(jnp.int32, (part_rows, 1), 0) // (heads * query_heads)
    lane = lax.broadcasted_iota(jnp.int32, (1, places), 1)
    for part in range(parts):
        for copy in copies[part]:
            copy.wait()
        query = query_ref[pl.ds(part * part_rows, part_rows), :]
        fresh_keys = fresh_ref[pl.ds(part * part_pairs, part_pairs), :]
        fresh = lax.dot_general(query, fresh_keys, contract, preferred_element_type=jnp.float32) * scale
        fresh = jnp.sum(jnp.where(own_fresh, fresh, 0.0), axis=1, keepdims=True)
        scores = []
        for block in range(blocks):
            base = (part * blocks + block) * slots
            keys = key_ref[pl.ds((part * blocks + block) * places, places), :]
            score = lax.dot_general(
                query[block * rows : (block + 1) * rows], keys, contract, preferred_element_type=jnp.float32
            )
            limit = jnp.full((1, places), lengths_ref[base], jnp.int32)
            for s in range(1, slots):
                limit = jnp.where(lane // (heads * context) == s, lengths_ref[base + s], limit)
            scores.append(jnp.where(own & (lane % context < limit), score * scale, NEGATIVE))
        scores = jnp.concatenate(scores, axis=0)
        top = jnp.maximum(jnp.max(scores, axis=1, keepdims=True), fresh)
        shares = jnp.exp(scores - top)
        fresh_share = jnp.exp(fresh - top)
        inverse = 1.0 / (jnp.sum(shares, axis=1, keepdims=True) + fresh_share)
        inverse = jnp.where(part * blocks * slots + row_slot < count_ref[0], inverse, 0.0)
        weights = (shares * inverse).astype(jnp.bfloat16)
        mixed = [
            jnp.dot(
                weights[block * rows : (block + 1) * rows],
                value_ref[pl.ds((part * blocks + block) * places, places), :],
                preferred_element_type=jnp.float32,
            )
            for block in range(blocks)
        ]
        mixed_ref[pl.ds(part * part_rows, part_rows), :] = jnp.concatenate(mixed, axis=0)
        share = jnp.where(own_fresh, fresh_share * inverse, 0.0)
        share_ref[pl.ds(part * part_rows, part_rows), :] = share.astype(share_ref.dtype)
        for write in writes[part]:
            write.start()
    for group_of_writes in writes:
        for write in group_of_writes:
            write.wait()


def cached_attention(query_rows, fresh_keys, cached_keys, cached_values, lengths, live_count):
    slots, heads, context, size = cached_keys.shape
    pairs = slots * heads
    query_heads = query_rows.shape[0] // pairs
    group, parts = 8, 4
    dims = (heads, query_heads, context, group, parts, 1.0 / math.sqrt(size))
    inputs = (
        query_rows,
        cached_keys.reshape(pairs * context, size),
        fresh_keys.reshape(pairs, size),
        cached_values.reshape(pairs * context, size),
    )
    outputs = [
        jax.ShapeDtypeStruct(query_rows.shape, jnp.float32),
        jax.ShapeDtypeStruct((query_rows.shape[0], pairs // parts), jnp.bfloat16),
    ]
    smem = pl.BlockSpec(memory_space=pltpu.SMEM)
    return pl.pallas_call(
        functools.partial(cached_kernel, dims),
        in_specs=[smem, smem] + [pl.BlockSpec(memory_space=pl.ANY)] * len(inputs),
        out_specs=[pl.BlockSpec(memory_space=pl.ANY)] * 2,
        out_shape=outputs,
        scratch_shapes=[pltpu.VMEM(x.shape, x.dtype) for x in (*inputs, *outputs)]
        + [pltpu.SemaphoreType.DMA((parts, len(inputs))), pltpu.SemaphoreType.DMA((parts, len(outputs)))],
        compiler_params=pltpu.CompilerParams(vmem_limit_bytes=56 << 20),
        cost_estimate=pl.CostEstimate(flops=1 << 28, bytes_accessed=6 << 20, transcendentals=1 << 18),
    )(lengths, live_count, *inputs)


def base_kernel(rows_ref, weight_ref, kept_ref, sent_ref):
    total = jnp.dot(rows_ref[...], weight_ref[...], preferred_element_type=jnp.float32)
    columns = kept_ref.shape[1]
    first = lax.axis_index("tensor") == 0
    kept_ref[...] = jnp.where(first, total[:, :columns], total[:, columns:])
    sent_ref[...] = jnp.where(first, total[:, columns:], total[:, :columns])


def base_sums(rows, weight):
    shape = jax.ShapeDtypeStruct((rows.shape[0], weight.shape[1] // 2), jnp.float32)
    vmem = pl.BlockSpec(memory_space=pltpu.VMEM)
    return pl.pallas_call(
        base_kernel,
        in_specs=[vmem, vmem],
        out_specs=[vmem, vmem],
        out_shape=[shape, shape],
        compiler_params=pltpu.CompilerParams(vmem_limit_bytes=8 << 20),
        cost_estimate=pl.CostEstimate(flops=1 << 28, bytes_accessed=3 << 20, transcendentals=0),
    )(rows, weight)


def final_kernel(count_ref, own_ref, returned_ref, mixed_ref, share_ref, attention_ref, values_ref, spread_ref):
    slots = own_ref.shape[0]
    pairs, size = values_ref.shape
    heads = pairs // slots
    live = lax.broadcasted_iota(jnp.int32, (slots, 1), 0) < count_ref[0]
    fresh = jnp.where(live, own_ref[...] + returned_ref[...].astype(jnp.float32), 0.0)
    for head in range(heads):
        spread_ref[pl.ds(head, slots, stride=heads), :] = fresh[:, head * size : (head + 1) * size]
    values = spread_ref[...].astype(jnp.bfloat16)
    values_ref[...] = values
    group = share_ref.shape[1]
    rows = group * attention_ref.shape[0] // pairs
    for block in range(pairs // group):
        part = pl.ds(block * rows, rows)
        fresh_part = jnp.dot(
            share_ref[part, :], values[block * group : (block + 1) * group], preferred_element_type=jnp.float32
        )
        attention_ref[part, :] = (mixed_ref[part, :] + fresh_part).astype(attention_ref.dtype)


def finish(own, returned, mixed, share, live_count):
    slots, columns = own.shape
    size = mixed.shape[1]
    pairs = slots * columns // size
    vmem = pl.BlockSpec(memory_space=pltpu.VMEM)
    return pl.pallas_call(
        final_kernel,
        in_specs=[pl.BlockSpec(memory_space=pltpu.SMEM), vmem, vmem, vmem, vmem],
        out_specs=[vmem, vmem],
        out_shape=[
            jax.ShapeDtypeStruct(mixed.shape, jnp.bfloat16),
            jax.ShapeDtypeStruct((pairs, size), jnp.bfloat16),
        ],
        scratch_shapes=[pltpu.VMEM((pairs, size), jnp.float32)],
        compiler_params=pltpu.CompilerParams(vmem_limit_bytes=8 << 20),
    )(live_count, own, returned, mixed, share)


def moved_delta(rows, down, up, homes, live_mask):
    slots, features = rows.shape
    replicas = lax.axis_size("replica")
    capacity = max(2, 2 * slots // replicas)
    index = jnp.arange(slots, dtype=jnp.int32)
    earlier = (homes[:, None] == homes[None, :]) & live_mask[None, :] & (index[None, :] < index[:, None])
    position = jnp.sum(earlier.astype(jnp.int32), axis=1)
    target = jnp.where(live_mask, homes * capacity + position, replicas * capacity)
    outgoing = jnp.zeros((replicas * capacity, features), jnp.bfloat16).at[target].set(rows, mode="drop")
    arrived = lax.all_to_all(outgoing, "replica", split_axis=0, concat_axis=0, tiled=True)
    part = jnp.einsum("nd,qd->nq", arrived, down, preferred_element_type=jnp.float32)
    shrunk = lax.psum(part, "tensor").astype(jnp.bfloat16)
    delta = jnp.dot(shrunk, up, preferred_element_type=jnp.float32)
    returned = lax.all_to_all(delta, "replica", split_axis=0, concat_axis=0, tiled=True)
    return jnp.take(returned, target, axis=0, mode="clip")


def home_masks(offsets, adapters, table_ref):
    homes = jnp.zeros(adapters.shape, jnp.int32)
    for adapter in range(table_ref.shape[0]):
        homes = jnp.where(adapters == adapter, table_ref[adapter], homes)
    place = lax.axis_index("replica")
    outer, inner = place // 2, place % 2
    return [homes == (outer ^ offset) * 2 + inner for offset in offsets]


def rank_kernel(offsets, half, table_ref, rows_ref, other_ref, adapters_ref, other_adapters_ref, down_ref, *rest):
    mine, theirs = rest[: len(offsets) - 1], rest[len(offsets) - 1 : -2]
    ranks_ref, panel_ref = rest[-2:]
    rank = 2 * half
    slots, features = rows_ref.shape
    start = lax.axis_index("group") * half
    panel_ref[pl.ds(0, rank), :] = down_ref[...]
    for k in range(1, len(offsets)):
        panel_ref[pl.ds(pl.multiple_of(k * rank + start, half), half), :] = mine[k - 1][:, :features]
        panel_ref[pl.ds(pl.multiple_of(k * rank + half - start, half), half), :] = theirs[k - 1][:, :features]
    contract = (((1,), (1,)), ((), ()))
    both = jnp.concatenate([rows_ref[...], other_ref[...]], axis=0)
    product = lax.dot_general(panel_ref[...], both, contract, preferred_element_type=jnp.float32)
    for i, adapters in enumerate((adapters_ref, other_adapters_ref)):
        total = jnp.zeros((rank, slots), jnp.float32)
        for k, here in enumerate(home_masks(offsets, adapters[...], table_ref)):
            total += jnp.where(here, product[k * rank : (k + 1) * rank, i * slots : (i + 1) * slots], 0.0)
        ranks_ref[pl.ds(i * rank, rank), :] = total


def delta_of(offsets, at, table_ref, adapters_ref, ranks_ref, got_ref, panel_ref):
    rank = ranks_ref.shape[0] // 2
    shrunk = ranks_ref[pl.ds(at * rank, rank), :] + got_ref[pl.ds(at * rank, rank), :]
    masks = home_masks(offsets, adapters_ref[...], table_ref)
    spread = jnp.concatenate([jnp.where(here, shrunk, 0.0) for here in masks], axis=0).astype(jnp.bfloat16)
    return lax.dot_general(spread, panel_ref[...], (((0,), (0,)), ((), ())), preferred_element_type=jnp.float32)


def sent_kernel(offsets, half, table_ref, adapters_ref, ranks_ref, got_ref, up_ref, *rest):
    mine, theirs = rest[: len(offsets) - 1], rest[len(offsets) - 1 : -2]
    sent_ref, panel_ref = rest[-2:]
    rank = 2 * half
    columns = sent_ref.shape[1]
    features = mine[0].shape[1] - columns
    start = lax.axis_index("group") * half
    panel_ref[pl.ds(0, rank), :] = up_ref[...]
    for k in range(1, len(offsets)):
        panel_ref[pl.ds(pl.multiple_of(k * rank + start, half), half), :] = mine[k - 1][:, features:]
        panel_ref[pl.ds(pl.multiple_of(k * rank + half - start, half), half), :] = theirs[k - 1][:, features:]
    sent_ref[...] = delta_of(offsets, 1, table_ref, adapters_ref, ranks_ref, got_ref, panel_ref).astype(sent_ref.dtype)


def own_kernel(offsets, table_ref, adapters_ref, ranks_ref, got_ref, panel_ref, kept_ref, base_ref, own_ref):
    delta = delta_of(offsets, 0, table_ref, adapters_ref, ranks_ref, got_ref, panel_ref)
    own_ref[...] = delta + (kept_ref[...] + base_ref[...])


def gathered_values(rows, weight, down, up, adapters, table, attention_inputs):
    slots, features = rows.shape
    rank, columns = up.shape
    replicas = lax.axis_size("replica")
    half = rank // 2
    adapters = adapters[None, :]
    vmem = pl.BlockSpec(memory_space=pltpu.VMEM)
    smem = pl.BlockSpec(memory_space=pltpu.SMEM)
    params = pltpu.CompilerParams(vmem_limit_bytes=16 << 20)
    start = lax.axis_index("group") * half
    packed = jnp.concatenate(
        [lax.dynamic_slice_in_dim(down, start, half, 0), lax.dynamic_slice_in_dim(up, start, half, 0)], axis=1
    )
    held = [(0, packed)]
    base_kept, base_sent = base_sums(rows, weight)
    other_adapters, sent_rows, base_sent = lax.optimization_barrier((swap(adapters, "replica", 1), rows, base_sent))
    other = swap(sent_rows, "replica", 1)
    near = swap(packed, "replica", 2)
    bit = replicas // 4
    while bit:
        came = [(offset ^ bit, swap(part, "replica", 2 * bit)) for offset, part in held if offset or bit > 1]
        if len(held) == 1:
            first, near, base_sent = lax.optimization_barrier((came[0][1], near, base_sent))
            came = [(came[0][0], first)]
        held = held + ([(1, near)] if bit == 1 else []) + came
        bit //= 2
    base_got = swap(base_sent, "tensor", 1)
    offsets = [offset for offset, _ in held]
    mine = [part for _, part in held[1:]]
    theirs = [swap(part, "group", 1) for part in mine]
    mine[-1], theirs[-2], query_rows = lax.optimization_barrier((mine[-1], theirs[-2], attention_inputs[0]))
    early = cached_attention(query_rows, *attention_inputs[1:])
    theirs[-1], early = lax.optimization_barrier((theirs[-1], early))
    inputs = [rows, other, adapters, other_adapters, down] + mine + theirs
    ranks = pl.pallas_call(
        functools.partial(rank_kernel, offsets, half),
        in_specs=[smem] + [vmem] * len(inputs),
        out_specs=vmem,
        out_shape=jax.ShapeDtypeStruct((2 * rank, slots), jnp.float32),
        scratch_shapes=[pltpu.VMEM((len(offsets) * rank, features), jnp.bfloat16)],
        compiler_params=params,
    )(table, *inputs)
    got = swap(ranks, "tensor", 1)
    inputs = [other_adapters, ranks, got, up] + mine + theirs
    sent, panel = pl.pallas_call(
        functools.partial(sent_kernel, offsets, half),
        in_specs=[smem] + [vmem] * len(inputs),
        out_specs=[vmem, vmem],
        out_shape=[
            jax.ShapeDtypeStruct((slots, columns), jnp.bfloat16),
            jax.ShapeDtypeStruct((len(offsets) * rank, columns), jnp.bfloat16),
        ],
        compiler_params=params,
    )(table, *inputs)
    returned = swap(sent, "replica", 1)
    inputs = [adapters, ranks, got, panel, base_kept, base_got]
    own = pl.pallas_call(
        functools.partial(own_kernel, offsets),
        in_specs=[smem] + [vmem] * len(inputs),
        out_specs=vmem,
        out_shape=jax.ShapeDtypeStruct((slots, columns), jnp.float32),
        compiler_params=params,
    )(table, *inputs)
    return own, returned, early


def local(
    hidden,
    queries,
    incoming_keys,
    stored_key_cache,
    stored_value_cache,
    base_value_weight,
    adapter_down_rows,
    adapter_up_rows,
    request_adapter,
    adapter_replica,
    replica_slot_count,
    cache_length,
):
    slots, _, features = hidden.shape
    heads, _, size = stored_key_cache.shape[1:]
    query_heads = queries.shape[3] // size
    replicas = lax.axis_size("replica")
    rows = hidden.reshape(slots, features)
    down, up = adapter_down_rows[0], adapter_up_rows[0]
    query_rows = queries.reshape(slots, heads, query_heads, size).transpose(0, 2, 1, 3).reshape(-1, size)
    attention_inputs = (
        query_rows, incoming_keys, stored_key_cache, stored_value_cache, cache_length, replica_slot_count
    )
    power = replicas >= 8 and replicas & (replicas - 1) == 0
    small = replicas * down.size <= GATHER_BYTES
    if power and small and lax.axis_size("group") == 2:
        own, returned, early = gathered_values(
            rows, base_value_weight, down, up, request_adapter, adapter_replica, attention_inputs
        )
    else:
        matches = request_adapter[:, None] == jnp.arange(adapter_replica.shape[0], dtype=jnp.int32)[None, :]
        homes = jnp.sum(jnp.where(matches, adapter_replica[None, :], 0), axis=1)
        live_mask = jnp.arange(slots, dtype=jnp.int32) < replica_slot_count[0]
        early = cached_attention(*attention_inputs)
        base_kept, base_sent = base_sums(rows, base_value_weight)
        own, returned = base_kept + swap(base_sent, "tensor", 1), moved_delta(rows, down, up, homes, live_mask)
    attention, fresh_values = finish(own, returned, *early, replica_slot_count)
    attention = attention.reshape(slots, query_heads, heads, size).transpose(0, 2, 1, 3)
    return (
        attention.reshape(slots, 1, heads, query_heads * size),
        fresh_values.reshape(slots, 1, heads, size),
    )


def solution(mesh):
    placed = (
        P(("group", "replica"), None, "tensor"),
        P(("group", "replica"), None, "tensor", None),
        P(("group", "replica"), None, "tensor", None),
        P(("group", "replica"), "tensor", None, None),
        P(("group", "replica"), "tensor", None, None),
        P("tensor", None),
        P("replica", None, "tensor"),
        P("replica", None, "tensor"),
        P("replica"),
        P(),
        P("replica"),
        P("replica"),
    )
    return jax.shard_map(
        local,
        mesh=mesh,
        in_specs=placed,
        out_specs=(
            P(("group", "replica"), None, "tensor", None),
            P(("group", "replica"), None, "tensor", None),
        ),
        check_vma=False,
    )
```

time: 40.9 us -> 37.1 us (0.907)
  waiting for transfers between devices: 11.8 us -> 7.55 us
  starting transfers between devices: 15.3 us -> 13.9 us
  local copies, waits for them, and re-layouts: 1.93 us -> 3.25 us
  Pallas kernels: 9.56 us -> 10.6 us
  other arithmetic: 0.68 us -> 0.01 us
    ppermute x14 -> x11, waiting for transfers between devices: 11.8 us -> 7.55 us  [swap(): return lax.ppermute(array, axis, [(i, i ^ bit) for i in range(size)])]
    ppermute x14 -> x11, starting transfers between devices: 15.3 us -> 13.9 us  [swap(): return lax.ppermute(array, axis, [(i, i ^ bit) for i in range(size)])]
    dynamic_slice x1 -> x2, local copies, waits for them, and re-layouts: 0.92 us -> 1.64 us  [the longest x1 0.91 us: gathered_values(): lax.dynamic_slice_in_dim(down, start, half, 0)]
    unnamed x16 -> x14, local copies, waits for them, and re-layouts: 0.92 us -> 1.62 us
    pallas_call x2 -> x4, Pallas kernels: 7.28 us -> 7.91 us  [the longest x1 4.92 us: cached_attention(): pl.pallas_call(functools.partial(cached_kernel, dims), in_specs=[smem, sm...]
    another operation x1 -> x0, other arithmetic: 0.59 us -> none  [local(): jnp.stack([replica_slot_count[0], lax.axis_index('tensor')])]
  transfers between devices with their start and end apart: 14 -> 11, of which waited for: 5 -> 4; matrix products, arithmetic and copies ran while one was open for 2% -> 0% of each run, Pallas kernels for 19% -> 26%
where the time goes in v2:
time: 37.1 us; the launch traced here: 36.8 us
  starting transfers between devices  13.9 us (37%)
  Pallas kernels  10.6 us (29%)
  waiting for transfers between devices  7.55 us (20%)
  local copies, waits for them, and re-layouts  3.25 us (9%)
  between operations  1.44 us (4%)
    ppermute x11, starting transfers between devices, swap(): return lax.ppermute(array, axis, [(i, i ^ bit) for i in range(size)])  13.9 us
    ppermute x11, waiting for transfers between devices, swap(): return lax.ppermute(array, axis, [(i, i ^ bit) for i in range(size)])  7.55 us
    pallas_call x1, Pallas kernels, cached_attention(): pl.pallas_call(functools.partial(cached_kernel, dims), in_specs=[smem, sm...  4.92 us
    pallas_call x1, Pallas kernels, gathered_values(): pl.pallas_call(functools.partial(rank_kernel, offsets, half), in_specs=[s...  1.66 us
    unnamed x14, local copies, waits for them, and re-layouts  1.62 us
    pallas_call x1, Pallas kernels, base_sums(): pl.pallas_call(base_kernel, in_specs=[vmem, vmem], out_specs=[vmem, vmem]...  1.5 us
    pallas_call x1, Pallas kernels, finish(): pl.pallas_call(final_kernel, in_specs=[pl.BlockSpec(memory_space=pltpu.SM...  1 us
    dynamic_slice x1, local copies, waits for them, and re-layouts, gathered_values(): lax.dynamic_slice_in_dim(down, start, half, 0)  0.91 us
  transfers between devices with their start and end apart: 11, of which 4 were waited for; matrix products, arithmetic and copies ran while one was open for 0% of the time, Pallas kernels for 26%

profile of v2, /device:TPU:0, one launch (start us, length us, event | category | flops | bytes accessed | tf_op | source)
XLA Modules:
  0.0 36.8 jit_solution(8789083936988791964)
XLA Ops:
  0.6 0.7 %dynamic-slice_bitcast_fusion.1 = bf16[32,256]{1,0:T(8,128)(2,1)S(1)} fusion(bf16[1,64,256]{2,1,0:T(8,128)(2,1)} %param.19, s32[]{:T(128)S(6)} %select_n.4), kind=kLoop, calls=%fused_computation.2 | loop fusion | bytes 32772 | tf_op jit(solution)/shard_map/dynamic_slice | solution.py:274
  1.4 0.9 %dynamic-slice_bitcast_fusion = bf16[32,2048]{1,0:T(8,128)(2,1)S(1)} fusion(bf16[1,64,2048]{2,1,0:T(8,128)(2,1)} %param.18, s32[]{:T(128)S(6)} %select_n.4), kind=kLoop, calls=%fused_computation.1 | loop fusion | bytes 262148 | tf_op jit(solution)/shard_map/dynamic_slice | solution.py:274
  2.3 3.1 %collective-permute-start.3 = (bf16[32,2304]{1,0:T(8,128)(2,1)S(1)}, bf16[32,2304]{1,0:T(8,128)(2,1)S(1)}, u32[]{:S(2)}, u32[]{:S(2)}) collective-permute-start(bf16[32,2304]{1,0:T(8,128)(2,1)S(1)} %pad_maximum_fusion), channel_id=1, source_target_pairs={{0,4},{2,6},{4,0},{6,2},{8,12},{10,14},{12,8},{14,10},{1,5},{3,7},... | collective-permute-start | bytes 442376 | tf_op jit(solution)/shard_map/ppermute | solution.py:17
  5.4 2.6 %collective-permute-start.2 = (bf16[32,2304]{1,0:T(8,128)(2,1)S(1)}, bf16[32,2304]{1,0:T(8,128)(2,1)S(1)}, u32[]{:S(2)}, u32[]{:S(2)}) collective-permute-start(bf16[32,2304]{1,0:T(8,128)(2,1)S(1)} %pad_maximum_fusion), channel_id=1, source_target_pairs={{0,8},{2,10},{4,12},{6,14},{8,0},{10,2},{12,4},{14,6},{1,9},{3,11}... | collective-permute-start | bytes 442376 | tf_op jit(solution)/shard_map/ppermute | solution.py:17
  8.0 1.5 %collective-permute-start = (s32[1,96]{1,0:T(1,128)}, s32[1,96]{1,0:T(1,128)S(1)}, u32[]{:S(2)}, u32[]{:S(2)}) collective-permute-start(s32[1,96]{1,0:T(1,128)} %bitcast.26), channel_id=1, source_target_pairs={{0,2},{2,0},{4,6},{6,4},{8,10},{10,8},{12,14},{14,12},{1,3},{3,1},... | collective-permute-start | bytes 1160 | tf_op jit(solution)/shard_map/ppermute | solution.py:17
  9.5 0.0 copy-start
  9.5 1.6 %copy-done = bf16[2048,512]{1,0:T(8,128)(2,1)S(1)} copy-done((bf16[2048,512]{1,0:T(8,128)(2,1)S(1)}, bf16[2048,512]{1,0:T(8,128)(2,1)}, u32[]{:S(2)}) %copy-start) | copy-done | bytes 2097176
  11.1 0.0 copy-start.2
  11.1 0.0 copy-start.5
  11.1 0.0 copy-start.6
  11.1 1.5 %shard_map.131 = (f32[96,256]{1,0:T(8,128)S(1)}, f32[96,256]{1,0:T(8,128)S(1)}) custom-call(bf16[96,2048]{1,0:T(8,128)(2,1)} %bitcast.1.rows_ref, bf16[2048,512]{1,0:T(8,128)(2,1)S(1)} %copy-done), custom_call_target="tpu_custom_call" | custom-call | flops 268435456 | bytes 3145728 | tf_op jit(solution)/shard_map/pallas_call | solution.py:142
  12.6 0.0 copy-start.4
  12.6 0.0 collective-permute-done.other_adapters_ref.adapters_ref
  12.6 0.6 %collective-permute-start.1 = (bf16[96,2048]{1,0:T(8,128)(2,1)}, bf16[96,2048]{1,0:T(8,128)(2,1)S(1)}, u32[]{:S(2)}, u32[]{:S(2)}) collective-permute-start(bf16[96,2048]{1,0:T(8,128)(2,1)} %bitcast.1.rows_ref), channel_id=1, source_target_pairs={{0,2},{2,0},{4,6},{6,4},{8,10},{10,8},{12,14},{14,12},{1,3},{3,1},... | collective-permute-start | bytes 1179656 | tf_op jit(solution)/shard_map/ppermute | solution.py:17
  13.2 0.0 collective-permute-done.3.rest_1_
  13.2 1.6 %collective-permute-done.2.rest_0_ = bf16[32,2304]{1,0:T(8,128)(2,1)S(1)} collective-permute-done((bf16[32,2304]{1,0:T(8,128)(2,1)S(1)}, bf16[32,2304]{1,0:T(8,128)(2,1)S(1)}, u32[]{:S(2)}, u32[]{:S(2)}) %collective-permute-start.2) | collective-permute-done | bytes 147488 | tf_op jit(solution)/shard_map/ppermute | solution.py:17
  14.8 0.4 %collective-permute-start.4 = (bf16[32,2304]{1,0:T(8,128)(2,1)S(1)}, bf16[32,2304]{1,0:T(8,128)(2,1)S(1)}, u32[]{:S(2)}, u32[]{:S(2)}) collective-permute-start(bf16[32,2304]{1,0:T(8,128)(2,1)S(1)} %collective-permute-done.2.rest_0_), channel_id=1, source_target_pairs={{0,4},{2,6},{4,0},{6,2},{8,12},{10,14},{12,8},{14,10},{1,5},{3,7},... | collective-permute-start | bytes 442376 | tf_op jit(solution)/shard_map/ppermute | solution.py:17
  15.2 1.5 %collective-permute-start.5 = (bf16[32,2304]{1,0:T(8,128)(2,1)S(1)}, bf16[32,2304]{1,0:T(8,128)(2,1)S(1)}, u32[]{:S(2)}, u32[]{:S(2)}) collective-permute-start(bf16[32,2304]{1,0:T(8,128)(2,1)S(1)} %collective-permute-done.3.rest_1_), channel_id=1, source_target_pairs={{0,16},{16,0},{1,17},{17,1},{2,18},{18,2},{3,19},{19,3},{4,20},{20... | collective-permute-start | bytes 442376 | tf_op jit(solution)/shard_map/ppermute | solution.py:17
  16.8 3.2 %collective-permute-done.4.rest_2_ = bf16[32,2304]{1,0:T(8,128)(2,1)S(1)} collective-permute-done((bf16[32,2304]{1,0:T(8,128)(2,1)S(1)}, bf16[32,2304]{1,0:T(8,128)(2,1)S(1)}, u32[]{:S(2)}, u32[]{:S(2)}) %collective-permute-start.4) | collective-permute-done | bytes 147488 | tf_op jit(solution)/shard_map/ppermute | solution.py:17
  19.9 1.5 %collective-permute-start.7 = (bf16[32,2304]{1,0:T(8,128)(2,1)S(1)}, bf16[32,2304]{1,0:T(8,128)(2,1)S(1)}, u32[]{:S(2)}, u32[]{:S(2)}) collective-permute-start(bf16[32,2304]{1,0:T(8,128)(2,1)S(1)} %collective-permute-done.4.rest_2_), channel_id=1, source_target_pairs={{0,16},{16,0},{1,17},{17,1},{2,18},{18,2},{3,19},{19,3},{4,20},{20... | collective-permute-start | bytes 442376 | tf_op jit(solution)/shard_map/ppermute | solution.py:17
  21.5 0.5 %collective-permute-start.6 = (bf16[32,2304]{1,0:T(8,128)(2,1)S(1)}, bf16[32,2304]{1,0:T(8,128)(2,1)S(1)}, u32[]{:S(2)}, u32[]{:S(2)}) collective-permute-start(bf16[32,2304]{1,0:T(8,128)(2,1)S(1)} %collective-permute-done.2.rest_0_), channel_id=1, source_target_pairs={{0,16},{16,0},{1,17},{17,1},{2,18},{18,2},{3,19},{19,3},{4,20},{20... | collective-permute-start | bytes 442376 | tf_op jit(solution)/shard_map/ppermute | solution.py:17
  22.6 0.1 collective-permute-start.9
  22.7 0.0 collective-permute-done.5.rest_4_
  22.7 4.9 %shard_map.132 = (f32[1536,128]{1,0:T(8,128)}, bf16[1536,48]{1,0:T(8,128)(2,1)}) custom-call(s32[96]{0:T(128)} %lengths_ref.1, s32[1]{0:T(128)S(6)} %copy.17.count_ref, bf16[1536,128]{1,0:T(8,128)(2,1)} %bitcast.31, bf16[3072,128]{1,0:T(8,128)(2,1)} %bitcast.29, bf16[192,128]{1,0:T(8,128)(2,1)} %bitcast.32, bf16[3072,128]{1,0:T(8,128)(2,1)} %bitcast.30), custom_call_target="tpu_custom_call" | custom-call | flops 268435456 | bytes 6291456 | tf_op jit(solution)/shard_map/pallas_call | solution.py:119
  27.6 0.0 copy-start.1
  27.6 0.0 copy-start.3
  27.7 0.0 collective-permute-done.7.rest_5_
  27.7 0.0 collective-permute-done.6.rest_3_
  27.7 0.0 collective-permute-done.1.other_ref
  27.7 0.0 copy-done.2
  27.7 0.0 copy-done.5
  27.7 0.0 copy-done.6
  27.7 1.7 %shard_map.133.ranks_ref = f32[128,96]{1,0:T(8,128)S(1)} custom-call(s32[8]{0:T(128)S(1)} %copy-done.5, bf16[96,2048]{1,0:T(8,128)(2,1)} %bitcast.1.rows_ref, bf16[96,2048]{1,0:T(8,128)(2,1)S(1)} %collective-permute-done.1.other_ref, s32[1,96]{1,0:T(1,128)S(1)} %bitcast.27, s32[1,96]{1,0:T(1,128)S(1)} %collective-permute-done.other_adapters_ref.adapters_ref, ...), custom_call_target="tpu_custom_call" | custom-call | tf_op jit(solution)/shard_map/pallas_call | solution.py:297
  29.4 0.6 %collective-permute-start.8 = (f32[128,96]{1,0:T(8,128)S(1)}, f32[128,96]{1,0:T(8,128)S(1)}, u32[]{:S(2)}, u32[]{:S(2)}) collective-permute-start(f32[128,96]{1,0:T(8,128)S(1)} %shard_map.133.ranks_ref), channel_id=1, source_target_pairs={{0,1},{1,0},{2,3},{3,2},{4,5},{5,4},{6,7},{7,6},{8,9},{9,8},{10,11... | collective-permute-start | bytes 147464 | tf_op jit(solution)/shard_map/ppermute | solution.py:17
  29.9 0.9 %collective-permute-done.8.got_ref = f32[128,96]{1,0:T(8,128)S(1)} collective-permute-done((f32[128,96]{1,0:T(8,128)S(1)}, f32[128,96]{1,0:T(8,128)S(1)}, u32[]{:S(2)}, u32[]{:S(2)}) %collective-permute-start.8) | collective-permute-done | bytes 49184 | tf_op jit(solution)/shard_map/ppermute | solution.py:17
  30.8 0.0 copy-done.4
  30.8 0.7 %shard_map.134 = (bf16[96,256]{1,0:T(8,128)(2,1)S(1)}, bf16[256,256]{1,0:T(8,128)(2,1)S(1)}) custom-call(s32[8]{0:T(128)S(1)} %copy-done.5, s32[1,96]{1,0:T(1,128)S(1)} %collective-permute-done.other_adapters_ref.adapters_ref, f32[128,96]{1,0:T(8,128)S(1)} %shard_map.133.ranks_ref, f32[128,96]{1,0:T(8,128)S(1)} %collective-permute-done.8.got_ref, ...), custom_call_target="tpu_custom_call" | custom-call | tf_op jit(solution)/shard_map/pallas_call | solution.py:307
  31.6 1.6 %collective-permute-start.10 = (bf16[96,256]{1,0:T(8,128)(2,1)S(1)}, bf16[96,256]{1,0:T(8,128)(2,1)S(1)}, u32[]{:S(2)}, u32[]{:S(2)}) collective-permute-start(bf16[96,256]{1,0:T(8,128)(2,1)S(1)} %get-tuple-element.37), channel_id=1, source_target_pairs={{0,2},{2,0},{4,6},{6,4},{8,10},{10,8},{12,14},{14,12},{1,3},{3,1},... | collective-permute-start | bytes 147464 | tf_op jit(solution)/shard_map/ppermute | solution.py:17
  33.1 0.0 collective-permute-done.9.base_ref
  33.1 0.7 %shard_map.135.own_ref = f32[96,256]{1,0:T(8,128)S(1)} custom-call(s32[8]{0:T(128)S(1)} %copy-done.5, s32[1,96]{1,0:T(1,128)S(1)} %bitcast.28, f32[128,96]{1,0:T(8,128)S(1)} %shard_map.133.ranks_ref, f32[128,96]{1,0:T(8,128)S(1)} %collective-permute-done.8.got_ref, bf16[256,256]{1,0:T(8,128)(2,1)S(1)} %get-tuple-element.34.panel_ref, ...), custom_call_target="tpu_custom_call" | custom-call | tf_op jit(solution)/shard_map/pallas_call | solution.py:319
  33.9 1.8 %collective-permute-done.10.returned_ref = bf16[96,256]{1,0:T(8,128)(2,1)S(1)} collective-permute-done((bf16[96,256]{1,0:T(8,128)(2,1)S(1)}, bf16[96,256]{1,0:T(8,128)(2,1)S(1)}, u32[]{:S(2)}, u32[]{:S(2)}) %collective-permute-start.10) | collective-permute-done | bytes 49184 | tf_op jit(solution)/shard_map/ppermute | solution.py:17
  35.7 0.0 copy-done.1
  35.7 0.0 copy-done.3
  35.8 1.0 %shard_map.136 = (bf16[1536,128]{1,0:T(8,128)(2,1)}, bf16[192,128]{1,0:T(8,128)(2,1)}) custom-call(s32[1]{0:T(128)S(6)} %copy.17.count_ref, f32[96,256]{1,0:T(8,128)S(1)} %shard_map.135.own_ref, bf16[96,256]{1,0:T(8,128)(2,1)S(1)} %collective-permute-done.10.returned_ref, f32[1536,128]{1,0:T(8,128)S(1)} %copy-done.1, bf16[1536,48]{1,0:T(8,128)(2,1)S(1)} %copy-done.3), custom_call_target="tpu_custom_call" | custom-call | tf_op jit(solution)/shard_map/pallas_call | solution.py:177
  (1 shorter events, 0.0 us)
Async XLA Ops:
  2.3 10.9 %collective-permute-start.3 = (bf16[32,2304]{1,0:T(8,128)(2,1)S(1)}, bf16[32,2304]{1,0:T(8,128)(2,1)S(1)}, u32[]{:S(2)}, u32[]{:S(2)}) collective-permute-start(bf16[32,2304]{1,0:T(8,128)(2,1)S(1)} %pad_maximum_fusion), channel_id=1, source_target_pairs={{0,4},{2,6},{4,0},{6,2},{8,12},{10,14},{12,8},{14,10},{1,5},{3,7},... | collective-permute-start | bytes 442376 | tf_op jit(solution)/shard_map/ppermute | solution.py:17
  5.4 9.4 %collective-permute-start.2 = (bf16[32,2304]{1,0:T(8,128)(2,1)S(1)}, bf16[32,2304]{1,0:T(8,128)(2,1)S(1)}, u32[]{:S(2)}, u32[]{:S(2)}) collective-permute-start(bf16[32,2304]{1,0:T(8,128)(2,1)S(1)} %pad_maximum_fusion), channel_id=1, source_target_pairs={{0,8},{2,10},{4,12},{6,14},{8,0},{10,2},{12,4},{14,6},{1,9},{3,11}... | collective-permute-start | bytes 442376 | tf_op jit(solution)/shard_map/ppermute | solution.py:17
  8.0 4.6 %collective-permute-start = (s32[1,96]{1,0:T(1,128)}, s32[1,96]{1,0:T(1,128)S(1)}, u32[]{:S(2)}, u32[]{:S(2)}) collective-permute-start(s32[1,96]{1,0:T(1,128)} %bitcast.26), channel_id=1, source_target_pairs={{0,2},{2,0},{4,6},{6,4},{8,10},{10,8},{12,14},{14,12},{1,3},{3,1},... | collective-permute-start | bytes 1160 | tf_op jit(solution)/shard_map/ppermute | solution.py:17
  9.5 1.6 %copy-start = (bf16[2048,512]{1,0:T(8,128)(2,1)S(1)}, bf16[2048,512]{1,0:T(8,128)(2,1)}, u32[]{:S(2)}) copy-start(bf16[2048,512]{1,0:T(8,128)(2,1)} %weight_ref.1) | copy-start | bytes 6291460
  11.1 16.6 %copy-start.2 = (bf16[1,64,2048]{2,1,0:T(8,128)(2,1)S(1)}, bf16[1,64,2048]{2,1,0:T(8,128)(2,1)}, u32[]{:S(2)}) copy-start(bf16[1,64,2048]{2,1,0:T(8,128)(2,1)} %param.18) | copy-start | bytes 786436
  11.1 16.6 %copy-start.5 = (s32[8]{0:T(128)S(1)}, s32[8]{0:T(128)}, u32[]{:S(2)}) copy-start(s32[8]{0:T(128)} %table_ref.5) | copy-start | bytes 100
  11.1 16.7 %copy-start.6 = (s32[96]{0:T(128)S(1)}, s32[96]{0:T(128)}, u32[]{:S(2)}) copy-start(s32[96]{0:T(128)} %param.20) | copy-start | bytes 1156
  12.6 18.3 %copy-start.4 = (bf16[1,64,256]{2,1,0:T(8,128)(2,1)S(1)}, bf16[1,64,256]{2,1,0:T(8,128)(2,1)}, u32[]{:S(2)}) copy-start(bf16[1,64,256]{2,1,0:T(8,128)(2,1)} %param.19) | copy-start | bytes 98308
  12.6 15.1 %collective-permute-start.1 = (bf16[96,2048]{1,0:T(8,128)(2,1)}, bf16[96,2048]{1,0:T(8,128)(2,1)S(1)}, u32[]{:S(2)}, u32[]{:S(2)}) collective-permute-start(bf16[96,2048]{1,0:T(8,128)(2,1)} %bitcast.1.rows_ref), channel_id=1, source_target_pairs={{0,2},{2,0},{4,6},{6,4},{8,10},{10,8},{12,14},{14,12},{1,3},{3,1},... | collective-permute-start | bytes 1179656 | tf_op jit(solution)/shard_map/ppermute | solution.py:17
  14.8 5.1 %collective-permute-start.4 = (bf16[32,2304]{1,0:T(8,128)(2,1)S(1)}, bf16[32,2304]{1,0:T(8,128)(2,1)S(1)}, u32[]{:S(2)}, u32[]{:S(2)}) collective-permute-start(bf16[32,2304]{1,0:T(8,128)(2,1)S(1)} %collective-permute-done.2.rest_0_), channel_id=1, source_target_pairs={{0,4},{2,6},{4,0},{6,2},{8,12},{10,14},{12,8},{14,10},{1,5},{3,7},... | collective-permute-start | bytes 442376 | tf_op jit(solution)/shard_map/ppermute | solution.py:17
  15.2 7.5 %collective-permute-start.5 = (bf16[32,2304]{1,0:T(8,128)(2,1)S(1)}, bf16[32,2304]{1,0:T(8,128)(2,1)S(1)}, u32[]{:S(2)}, u32[]{:S(2)}) collective-permute-start(bf16[32,2304]{1,0:T(8,128)(2,1)S(1)} %collective-permute-done.3.rest_1_), channel_id=1, source_target_pairs={{0,16},{16,0},{1,17},{17,1},{2,18},{18,2},{3,19},{19,3},{4,20},{20... | collective-permute-start | bytes 442376 | tf_op jit(solution)/shard_map/ppermute | solution.py:17
  19.9 7.7 %collective-permute-start.7 = (bf16[32,2304]{1,0:T(8,128)(2,1)S(1)}, bf16[32,2304]{1,0:T(8,128)(2,1)S(1)}, u32[]{:S(2)}, u32[]{:S(2)}) collective-permute-start(bf16[32,2304]{1,0:T(8,128)(2,1)S(1)} %collective-permute-done.4.rest_2_), channel_id=1, source_target_pairs={{0,16},{16,0},{1,17},{17,1},{2,18},{18,2},{3,19},{19,3},{4,20},{20... | collective-permute-start | bytes 442376 | tf_op jit(solution)/shard_map/ppermute | solution.py:17
  21.5 6.2 %collective-permute-start.6 = (bf16[32,2304]{1,0:T(8,128)(2,1)S(1)}, bf16[32,2304]{1,0:T(8,128)(2,1)S(1)}, u32[]{:S(2)}, u32[]{:S(2)}) collective-permute-start(bf16[32,2304]{1,0:T(8,128)(2,1)S(1)} %collective-permute-done.2.rest_0_), channel_id=1, source_target_pairs={{0,16},{16,0},{1,17},{17,1},{2,18},{18,2},{3,19},{19,3},{4,20},{20... | collective-permute-start | bytes 442376 | tf_op jit(solution)/shard_map/ppermute | solution.py:17
  22.6 10.5 %collective-permute-start.9 = (f32[96,256]{1,0:T(8,128)S(1)}, f32[96,256]{1,0:T(8,128)S(1)}, u32[]{:S(2)}, u32[]{:S(2)}) collective-permute-start(f32[96,256]{1,0:T(8,128)S(1)} %get-tuple-element.36), channel_id=1, source_target_pairs={{0,1},{1,0},{2,3},{3,2},{4,5},{5,4},{6,7},{7,6},{8,9},{9,8},{10,11... | collective-permute-start | bytes 294920 | tf_op jit(solution)/shard_map/ppermute | solution.py:17
  27.6 8.1 %copy-start.1 = (f32[1536,128]{1,0:T(8,128)S(1)}, f32[1536,128]{1,0:T(8,128)}, u32[]{:S(2)}) copy-start(f32[1536,128]{1,0:T(8,128)} %get-tuple-element.38.mixed_ref) | copy-start | bytes 2359300
  27.6 8.1 %copy-start.3 = (bf16[1536,48]{1,0:T(8,128)(2,1)S(1)}, bf16[1536,48]{1,0:T(8,128)(2,1)}, u32[]{:S(2)}) copy-start(bf16[1536,48]{1,0:T(8,128)(2,1)} %get-tuple-element.39.share_ref) | copy-start | bytes 442372
  29.4 1.5 %collective-permute-start.8 = (f32[128,96]{1,0:T(8,128)S(1)}, f32[128,96]{1,0:T(8,128)S(1)}, u32[]{:S(2)}, u32[]{:S(2)}) collective-permute-start(f32[128,96]{1,0:T(8,128)S(1)} %shard_map.133.ranks_ref), channel_id=1, source_target_pairs={{0,1},{1,0},{2,3},{3,2},{4,5},{5,4},{6,7},{7,6},{8,9},{9,8},{10,11... | collective-permute-start | bytes 147464 | tf_op jit(solution)/shard_map/ppermute | solution.py:17
  31.6 4.2 %collective-permute-start.10 = (bf16[96,256]{1,0:T(8,128)(2,1)S(1)}, bf16[96,256]{1,0:T(8,128)(2,1)S(1)}, u32[]{:S(2)}, u32[]{:S(2)}) collective-permute-start(bf16[96,256]{1,0:T(8,128)(2,1)S(1)} %get-tuple-element.37), channel_id=1, source_target_pairs={{0,2},{2,0},{4,6},{6,4},{8,10},{10,8},{12,14},{14,12},{1,3},{3,1},... | collective-permute-start | bytes 147464 | tf_op jit(solution)/shard_map/ppermute | solution.py:17

commit v3 on v2

--- a/solution.py
+++ b/solution.py
@@ -18,14 +18,14 @@
 
 
 def cached_kernel(dims, lengths_ref, count_ref, *refs):
-    heads, query_heads, context, group, parts, scale = dims
+    heads, query_heads, context, group, parts, opening, scale = dims
     sources, outputs, buffers, results = refs[:4], refs[4:6], refs[6:10], refs[10:12]
     in_sems, out_sems = refs[12:]
 
     def copy_of(source, target, sem, part):
-        size = source.shape[0] // parts
-        at = pl.ds(part * size, size)
-        return pltpu.make_async_copy(source.at[at], target.at[at], sem)
+        size = min(source.shape[0], target.shape[0]) // parts
+        begin = [(opening + part if ref.shape[0] > size * parts else part) * size for ref in (source, target)]
+        return pltpu.make_async_copy(source.at[pl.ds(begin[0], size)], target.at[pl.ds(begin[1], size)], sem)
 
     copies = [
         [copy_of(source, buffer, in_sems.at[part, i], part) for i, (source, buffer) in enumerate(zip(sources, buffers))]
@@ -65,7 +65,7 @@
         fresh = jnp.sum(jnp.where(own_fresh, fresh, 0.0), axis=1, keepdims=True)
         scores = []
         for block in range(blocks):
-            base = (part * blocks + block) * slots
+            base = ((opening + part) * blocks + block) * slots
             keys = key_ref[pl.ds((part * blocks + block) * places, places), :]
             score = lax.dot_general(
                 query[block * rows : (block + 1) * rows], keys, contract, preferred_element_type=jnp.float32
@@ -79,7 +79,7 @@
         shares = jnp.exp(scores - top)
         fresh_share = jnp.exp(fresh - top)
         inverse = 1.0 / (jnp.sum(shares, axis=1, keepdims=True) + fresh_share)
-        inverse = jnp.where(part * blocks * slots + row_slot < count_ref[0], inverse, 0.0)
+        inverse = jnp.where((opening + part) * blocks * slots + row_slot < count_ref[0], inverse, 0.0)
         weights = (shares * inverse).astype(jnp.bfloat16)
         mixed = [
             jnp.dot(
@@ -99,21 +99,22 @@
             write.wait()
 
 
-def cached_attention(query_rows, fresh_keys, cached_keys, cached_values, lengths, live_count):
+def cached_attention(opening, parts, query_rows, fresh_keys, cached_keys, cached_values, lengths, live_count):
     slots, heads, context, size = cached_keys.shape
     pairs = slots * heads
     query_heads = query_rows.shape[0] // pairs
-    group, parts = 8, 4
-    dims = (heads, query_heads, context, group, parts, 1.0 / math.sqrt(size))
+    group, runs = 8, 2
+    dims = (heads, query_heads, context, group, parts, opening, 1.0 / math.sqrt(size))
     inputs = (
         query_rows,
         cached_keys.reshape(pairs * context, size),
         fresh_keys.reshape(pairs, size),
         cached_values.reshape(pairs * context, size),
     )
+    rows = query_rows.shape[0] // runs * parts
     outputs = [
-        jax.ShapeDtypeStruct(query_rows.shape, jnp.float32),
-        jax.ShapeDtypeStruct((query_rows.shape[0], pairs // parts), jnp.bfloat16),
+        jax.ShapeDtypeStruct((rows, size), jnp.float32),
+        jax.ShapeDtypeStruct((rows, pairs // runs), jnp.bfloat16),
     ]
     smem = pl.BlockSpec(memory_space=pltpu.SMEM)
     return pl.pallas_call(
@@ -121,14 +122,16 @@
         in_specs=[smem, smem] + [pl.BlockSpec(memory_space=pl.ANY)] * len(inputs),
         out_specs=[pl.BlockSpec(memory_space=pl.ANY)] * 2,
         out_shape=outputs,
-        scratch_shapes=[pltpu.VMEM(x.shape, x.dtype) for x in (*inputs, *outputs)]
+        scratch_shapes=[pltpu.VMEM((x.shape[0] // runs * parts, x.shape[1]), x.dtype) for x in inputs]
+        + [pltpu.VMEM(x.shape, x.dtype) for x in outputs]
         + [pltpu.SemaphoreType.DMA((parts, len(inputs))), pltpu.SemaphoreType.DMA((parts, len(outputs)))],
         compiler_params=pltpu.CompilerParams(vmem_limit_bytes=56 << 20),
-        cost_estimate=pl.CostEstimate(flops=1 << 28, bytes_accessed=6 << 20, transcendentals=1 << 18),
+        cost_estimate=pl.CostEstimate(flops=1 << 26, bytes_accessed=3 << 20, transcendentals=1 << 17),
     )(lengths, live_count, *inputs)
 
 
-def base_kernel(rows_ref, weight_ref, kept_ref, sent_ref):
+def base_kernel(rows_ref, weight_ref, kept_ref, sent_ref, copy_ref):
+    copy_ref[...] = rows_ref[...]
     total = jnp.dot(rows_ref[...], weight_ref[...], preferred_element_type=jnp.float32)
     columns = kept_ref.shape[1]
     first = lax.axis_index("tensor") == 0
@@ -142,14 +145,15 @@
     return pl.pallas_call(
         base_kernel,
         in_specs=[vmem, vmem],
-        out_specs=[vmem, vmem],
-        out_shape=[shape, shape],
+        out_specs=[vmem, vmem, vmem],
+        out_shape=[shape, shape, jax.ShapeDtypeStruct(rows.shape, rows.dtype)],
         compiler_params=pltpu.CompilerParams(vmem_limit_bytes=8 << 20),
         cost_estimate=pl.CostEstimate(flops=1 << 28, bytes_accessed=3 << 20, transcendentals=0),
     )(rows, weight)
 
 
-def final_kernel(count_ref, own_ref, returned_ref, mixed_ref, share_ref, attention_ref, values_ref, spread_ref):
+def final_kernel(count_ref, own_ref, returned_ref, *rest):
+    halves, (attention_ref, values_ref, spread_ref) = rest[:-3], rest[-3:]
     slots = own_ref.shape[0]
     pairs, size = values_ref.shape
     heads = pairs // slots
@@ -159,32 +163,36 @@
         spread_ref[pl.ds(head, slots, stride=heads), :] = fresh[:, head * size : (head + 1) * size]
     values = spread_ref[...].astype(jnp.bfloat16)
     values_ref[...] = values
-    group = share_ref.shape[1]
-    rows = group * attention_ref.shape[0] // pairs
-    for block in range(pairs // group):
-        part = pl.ds(block * rows, rows)
-        fresh_part = jnp.dot(
-            share_ref[part, :], values[block * group : (block + 1) * group], preferred_element_type=jnp.float32
-        )
-        attention_ref[part, :] = (mixed_ref[part, :] + fresh_part).astype(attention_ref.dtype)
-
-
-def finish(own, returned, mixed, share, live_count):
+    done = 0
+    for mixed_ref, share_ref in zip(halves[::2], halves[1::2]):
+        group = share_ref.shape[1]
+        rows = group * attention_ref.shape[0] // pairs
+        for begin in range(0, mixed_ref.shape[0], rows):
+            fresh_part = jnp.dot(
+                share_ref[pl.ds(begin, rows), :], values[done : done + group], preferred_element_type=jnp.float32
+            )
+            attended = mixed_ref[pl.ds(begin, rows), :] + fresh_part
+            attention_ref[pl.ds(done // group * rows, rows), :] = attended.astype(attention_ref.dtype)
+            done += group
+
+
+def finish(own, returned, halves, live_count):
     slots, columns = own.shape
-    size = mixed.shape[1]
+    size = halves[0].shape[1]
     pairs = slots * columns // size
+    query_rows = sum(half.shape[0] for half in halves[::2])
     vmem = pl.BlockSpec(memory_space=pltpu.VMEM)
     return pl.pallas_call(
         final_kernel,
-        in_specs=[pl.BlockSpec(memory_space=pltpu.SMEM), vmem, vmem, vmem, vmem],
+        in_specs=[pl.BlockSpec(memory_space=pltpu.SMEM), vmem, vmem] + [vmem] * len(halves),
         out_specs=[vmem, vmem],
         out_shape=[
-            jax.ShapeDtypeStruct(mixed.shape, jnp.bfloat16),
+            jax.ShapeDtypeStruct((query_rows, size), jnp.bfloat16),
             jax.ShapeDtypeStruct((pairs, size), jnp.bfloat16),
         ],
         scratch_shapes=[pltpu.VMEM((pairs, size), jnp.float32)],
         compiler_params=pltpu.CompilerParams(vmem_limit_bytes=8 << 20),
-    )(live_count, own, returned, mixed, share)
+    )(live_count, own, returned, *halves)
 
 
 def moved_delta(rows, down, up, homes, live_mask):
@@ -213,16 +221,22 @@
     return [homes == (outer ^ offset) * 2 + inner for offset in offsets]
 
 
-def rank_kernel(offsets, half, table_ref, rows_ref, other_ref, adapters_ref, other_adapters_ref, down_ref, *rest):
-    mine, theirs = rest[: len(offsets) - 1], rest[len(offsets) - 1 : -2]
+def fill(panel_ref, columns, half, wholes, mine, theirs):
+    rank = 2 * half
+    start = lax.axis_index("group") * half
+    for k, whole in enumerate(wholes):
+        panel_ref[pl.ds(k * rank, rank), :] = whole[:, columns] if whole.shape[1] > panel_ref.shape[1] else whole[...]
+    for k, (first, second) in enumerate(zip(mine, theirs), len(wholes)):
+        panel_ref[pl.ds(pl.multiple_of(k * rank + start, half), half), :] = first[:, columns]
+        panel_ref[pl.ds(pl.multiple_of(k * rank + half - start, half), half), :] = second[:, columns]
+
+
+def rank_kernel(offsets, half, counts, table_ref, rows_ref, other_ref, adapters_ref, other_adapters_ref, *rest):
+    wholes, mine, theirs = rest[: counts[0]], rest[counts[0] : sum(counts)], rest[sum(counts) : -2]
     ranks_ref, panel_ref = rest[-2:]
     rank = 2 * half
     slots, features = rows_ref.shape
-    start = lax.axis_index("group") * half
-    panel_ref[pl.ds(0, rank), :] = down_ref[...]
-    for k in range(1, len(offsets)):
-        panel_ref[pl.ds(pl.multiple_of(k * rank + start, half), half), :] = mine[k - 1][:, :features]
-        panel_ref[pl.ds(pl.multiple_of(k * rank + half - start, half), half), :] = theirs[k - 1][:, :features]
+    fill(panel_ref, slice(0, features), half, wholes, mine, theirs)
     contract = (((1,), (1,)), ((), ()))
     both = jnp.concatenate([rows_ref[...], other_ref[...]], axis=0)
     product = lax.dot_general(panel_ref[...], both, contract, preferred_element_type=jnp.float32)
@@ -241,17 +255,11 @@
     return lax.dot_general(spread, panel_ref[...], (((0,), (0,)), ((), ())), preferred_element_type=jnp.float32)
 
 
-def sent_kernel(offsets, half, table_ref, adapters_ref, ranks_ref, got_ref, up_ref, *rest):
-    mine, theirs = rest[: len(offsets) - 1], rest[len(offsets) - 1 : -2]
+def sent_kernel(offsets, half, counts, table_ref, adapters_ref, ranks_ref, got_ref, *rest):
+    wholes, mine, theirs = rest[: counts[0]], rest[counts[0] : sum(counts)], rest[sum(counts) : -2]
     sent_ref, panel_ref = rest[-2:]
-    rank = 2 * half
-    columns = sent_ref.shape[1]
-    features = mine[0].shape[1] - columns
-    start = lax.axis_index("group") * half
-    panel_ref[pl.ds(0, rank), :] = up_ref[...]
-    for k in range(1, len(offsets)):
-        panel_ref[pl.ds(pl.multiple_of(k * rank + start, half), half), :] = mine[k - 1][:, features:]
-        panel_ref[pl.ds(pl.multiple_of(k * rank + half - start, half), half), :] = theirs[k - 1][:, features:]
+    width = mine[0].shape[1]
+    fill(panel_ref, slice(width - sent_ref.shape[1], width), half, wholes, mine, theirs)
     sent_ref[...] = delta_of(offsets, 1, table_ref, adapters_ref, ranks_ref, got_ref, panel_ref).astype(sent_ref.dtype)
 
 
@@ -273,29 +281,31 @@
     packed = jnp.concatenate(
         [lax.dynamic_slice_in_dim(down, start, half, 0), lax.dynamic_slice_in_dim(up, start, half, 0)], axis=1
     )
-    held = [(0, packed)]
-    base_kept, base_sent = base_sums(rows, weight)
+    base_kept, base_sent, rows_near = base_sums(rows, weight)
     other_adapters, sent_rows, base_sent = lax.optimization_barrier((swap(adapters, "replica", 1), rows, base_sent))
     other = swap(sent_rows, "replica", 1)
-    near = swap(packed, "replica", 2)
+    near = swap(jnp.concatenate([down, up], axis=1), "replica", 2)
+    query_rows, *attention_rest = attention_inputs
+    held = [(0, packed)]
     bit = replicas // 4
     while bit:
         came = [(offset ^ bit, swap(part, "replica", 2 * bit)) for offset, part in held if offset or bit > 1]
         if len(held) == 1:
-            first, near, base_sent = lax.optimization_barrier((came[0][1], near, base_sent))
+            first, base_sent, query_rows = lax.optimization_barrier((came[0][1], base_sent, query_rows))
             came = [(came[0][0], first)]
-        held = held + ([(1, near)] if bit == 1 else []) + came
+        held = held + came
         bit //= 2
     base_got = swap(base_sent, "tensor", 1)
-    offsets = [offset for offset, _ in held]
+    offsets = [0, 1] + [offset for offset, _ in held[1:]]
     mine = [part for _, part in held[1:]]
     theirs = [swap(part, "group", 1) for part in mine]
-    mine[-1], theirs[-2], query_rows = lax.optimization_barrier((mine[-1], theirs[-2], attention_inputs[0]))
-    early = cached_attention(query_rows, *attention_inputs[1:])
-    theirs[-1], early = lax.optimization_barrier((theirs[-1], early))
-    inputs = [rows, other, adapters, other_adapters, down] + mine + theirs
+    mine[-1], theirs[-2], query_rows = lax.optimization_barrier((mine[-1], theirs[-2], query_rows))
+    halves = cached_attention(0, 2, query_rows, *attention_rest)
+
+    theirs[-1], halves = lax.optimization_barrier((theirs[-1], halves))
+    inputs = [rows_near, other, adapters, other_adapters, down, near] + mine + theirs
     ranks = pl.pallas_call(
-        functools.partial(rank_kernel, offsets, half),
+        functools.partial(rank_kernel, offsets, half, (2, len(mine))),
         in_specs=[smem] + [vmem] * len(inputs),
         out_specs=vmem,
         out_shape=jax.ShapeDtypeStruct((2 * rank, slots), jnp.float32),
@@ -303,9 +313,9 @@
         compiler_params=params,
     )(table, *inputs)
     got = swap(ranks, "tensor", 1)
-    inputs = [other_adapters, ranks, got, up] + mine + theirs
+    inputs = [other_adapters, ranks, got, up, near] + mine + theirs
     sent, panel = pl.pallas_call(
-        functools.partial(sent_kernel, offsets, half),
+        functools.partial(sent_kernel, offsets, half, (2, len(mine))),
         in_specs=[smem] + [vmem] * len(inputs),
         out_specs=[vmem, vmem],
         out_shape=[
@@ -323,7 +333,7 @@
         out_shape=jax.ShapeDtypeStruct((slots, columns), jnp.float32),
         compiler_params=params,
     )(table, *inputs)
-    return own, returned, early
+    return own, returned, halves
 
 
 def local(
@@ -353,17 +363,17 @@
     power = replicas >= 8 and replicas & (replicas - 1) == 0
     small = replicas * down.size <= GATHER_BYTES
     if power and small and lax.axis_size("group") == 2:
-        own, returned, early = gathered_values(
+        own, returned, halves = gathered_values(
             rows, base_value_weight, down, up, request_adapter, adapter_replica, attention_inputs
         )
     else:
         matches = request_adapter[:, None] == jnp.arange(adapter_replica.shape[0], dtype=jnp.int32)[None, :]
         homes = jnp.sum(jnp.where(matches, adapter_replica[None, :], 0), axis=1)
         live_mask = jnp.arange(slots, dtype=jnp.int32) < replica_slot_count[0]
-        early = cached_attention(*attention_inputs)
-        base_kept, base_sent = base_sums(rows, base_value_weight)
+        halves = cached_attention(0, 2, *attention_inputs)
+        base_kept, base_sent, _ = base_sums(rows, base_value_weight)
         own, returned = base_kept + swap(base_sent, "tensor", 1), moved_delta(rows, down, up, homes, live_mask)
-    attention, fresh_values = finish(own, returned, *early, replica_slot_count)
+    attention, fresh_values = finish(own, returned, halves, replica_slot_count)
     attention = attention.reshape(slots, query_heads, heads, size).transpose(0, 2, 1, 3)
     return (
         attention.reshape(slots, 1, heads, query_heads * size),

time: 37.1 us -> 35.7 us (0.962)
  Pallas kernels: 10.6 us -> 9.38 us
    pallas_call x1, Pallas kernels: 4.92 us -> 4.28 us  [cached_attention(): pl.pallas_call(functools.partial(cached_kernel, dims), in_specs=[smem, sm...]
    pallas_call x3, Pallas kernels: 3.91 us -> 3.35 us  [the longest x1 1.51 us: base_sums(): pl.pallas_call(base_kernel, in_specs=[vmem, vmem], out_specs=[vmem, vmem,...]
    ppermute x11 -> x10, starting transfers between devices: 13.9 us -> 13.6 us  [swap(): return lax.ppermute(array, axis, [(i, i ^ bit) for i in range(size)])]
    ppermute x11 -> x10, waiting for transfers between devices: 7.55 us -> 7.65 us  [swap(): return lax.ppermute(array, axis, [(i, i ^ bit) for i in range(size)])]
  transfers between devices with their start and end apart: 11 -> 10, of which waited for: 4 -> 4; matrix products, arithmetic and copies ran while one was open for 0% -> 0% of each run, Pallas kernels for 26% -> 24%
where the time goes in v3:
time: 35.7 us; the launch traced here: 35.4 us
  starting transfers between devices  13.6 us (38%)
  Pallas kernels  9.38 us (26%)
  waiting for transfers between devices  7.65 us (21%)
  local copies, waits for them, and re-layouts  3.3 us (9%)
  between operations  1.44 us (4%)
    ppermute x10, starting transfers between devices, swap(): return lax.ppermute(array, axis, [(i, i ^ bit) for i in range(size)])  13.6 us
    ppermute x10, waiting for transfers between devices, swap(): return lax.ppermute(array, axis, [(i, i ^ bit) for i in range(size)])  7.65 us
    pallas_call x1, Pallas kernels, cached_attention(): pl.pallas_call(functools.partial(cached_kernel, dims), in_specs=[smem, sm...  4.28 us
    unnamed x14, local copies, waits for them, and re-layouts  1.62 us
    pallas_call x1, Pallas kernels, base_sums(): pl.pallas_call(base_kernel, in_specs=[vmem, vmem], out_specs=[vmem, vmem,...  1.51 us
    pallas_call x1, Pallas kernels, gathered_values(): pl.pallas_call(functools.partial(rank_kernel, offsets, half, (2, len(mine...  1.09 us
    pallas_call x1, Pallas kernels, finish(): pl.pallas_call(final_kernel, in_specs=[pl.BlockSpec(memory_space=pltpu.SM...  1.01 us
    dynamic_slice x1, local copies, waits for them, and re-layouts, gathered_values(): lax.dynamic_slice_in_dim(down, start, half, 0)  0.91 us
  transfers between devices with their start and end apart: 10, of which 4 were waited for; matrix products, arithmetic and copies ran while one was open for 0% of the time, Pallas kernels for 24%

profile of v3, /device:TPU:0, one launch (start us, length us, event | category | flops | bytes accessed | tf_op | source)
XLA Modules:
  0.0 35.4 jit_solution(11592536088049065283)
XLA Ops:
  0.6 0.0 copy-start.4
  0.6 0.0 copy-start.1
  0.7 0.8 %dynamic-slice_bitcast_fusion.1 = bf16[32,256]{1,0:T(8,128)(2,1)S(1)} fusion(bf16[1,64,256]{2,1,0:T(8,128)(2,1)} %param.19, s32[]{:T(128)S(6)} %select_n.4), kind=kLoop, calls=%fused_computation.3 | loop fusion | bytes 32772 | tf_op jit(solution)/shard_map/dynamic_slice | solution.py:282
  1.4 0.9 %dynamic-slice_bitcast_fusion = bf16[32,2048]{1,0:T(8,128)(2,1)S(1)} fusion(bf16[1,64,2048]{2,1,0:T(8,128)(2,1)} %param.18, s32[]{:T(128)S(6)} %select_n.4), kind=kLoop, calls=%fused_computation.2 | loop fusion | bytes 262148 | tf_op jit(solution)/shard_map/dynamic_slice | solution.py:282
  2.4 4.1 %collective-permute-start.3 = (bf16[32,2304]{1,0:T(8,128)(2,1)S(1)}, bf16[32,2304]{1,0:T(8,128)(2,1)S(1)}, u32[]{:S(2)}, u32[]{:S(2)}) collective-permute-start(bf16[32,2304]{1,0:T(8,128)(2,1)S(1)} %pad_maximum_fusion.1), channel_id=1, source_target_pairs={{0,8},{2,10},{4,12},{6,14},{8,0},{10,2},{12,4},{14,6},{1,9},{3,11}... | collective-permute-start | bytes 442376 | tf_op jit(solution)/shard_map/ppermute | solution.py:17
  6.5 1.5 %collective-permute-start = (s32[1,96]{1,0:T(1,128)}, s32[1,96]{1,0:T(1,128)S(1)}, u32[]{:S(2)}, u32[]{:S(2)}) collective-permute-start(s32[1,96]{1,0:T(1,128)} %bitcast.28), channel_id=1, source_target_pairs={{0,2},{2,0},{4,6},{6,4},{8,10},{10,8},{12,14},{14,12},{1,3},{3,1},... | collective-permute-start | bytes 1160 | tf_op jit(solution)/shard_map/ppermute | solution.py:17
  8.0 0.0 copy-start
  8.0 1.6 %copy-done = bf16[2048,512]{1,0:T(8,128)(2,1)S(1)} copy-done((bf16[2048,512]{1,0:T(8,128)(2,1)S(1)}, bf16[2048,512]{1,0:T(8,128)(2,1)}, u32[]{:S(2)}) %copy-start) | copy-done | bytes 2097176
  9.5 0.0 copy-start.5
  9.5 0.0 copy-start.6
  9.5 1.5 %shard_map.131 = (f32[96,256]{1,0:T(8,128)S(1)}, f32[96,256]{1,0:T(8,128)S(1)}, bf16[96,2048]{1,0:T(8,128)(2,1)S(1)}) custom-call(bf16[96,2048]{1,0:T(8,128)(2,1)} %bitcast.1.rows_ref, bf16[2048,512]{1,0:T(8,128)(2,1)S(1)} %copy-done), custom_call_target="tpu_custom_call" | custom-call | flops 268435456 | bytes 3145728 | tf_op jit(solution)/shard_map/pallas_call | solution.py:145
  11.1 0.0 collective-permute-done.other_adapters_ref.adapters_ref
  11.1 0.6 %collective-permute-start.1 = (bf16[96,2048]{1,0:T(8,128)(2,1)}, bf16[96,2048]{1,0:T(8,128)(2,1)S(1)}, u32[]{:S(2)}, u32[]{:S(2)}) collective-permute-start(bf16[96,2048]{1,0:T(8,128)(2,1)} %bitcast.1.rows_ref), channel_id=1, source_target_pairs={{0,2},{2,0},{4,6},{6,4},{8,10},{10,8},{12,14},{14,12},{1,3},{3,1},... | collective-permute-start | bytes 1179656 | tf_op jit(solution)/shard_map/ppermute | solution.py:17
  11.7 1.8 %collective-permute-done.3.rest_2_ = bf16[32,2304]{1,0:T(8,128)(2,1)S(1)} collective-permute-done((bf16[32,2304]{1,0:T(8,128)(2,1)S(1)}, bf16[32,2304]{1,0:T(8,128)(2,1)S(1)}, u32[]{:S(2)}, u32[]{:S(2)}) %collective-permute-start.3) | collective-permute-done | bytes 147488 | tf_op jit(solution)/shard_map/ppermute | solution.py:17
  13.5 0.7 %collective-permute-start.4 = (bf16[32,2304]{1,0:T(8,128)(2,1)S(1)}, bf16[32,2304]{1,0:T(8,128)(2,1)S(1)}, u32[]{:S(2)}, u32[]{:S(2)}) collective-permute-start(bf16[32,2304]{1,0:T(8,128)(2,1)S(1)} %collective-permute-done.3.rest_2_), channel_id=1, source_target_pairs={{0,4},{2,6},{4,0},{6,2},{8,12},{10,14},{12,8},{14,10},{1,5},{3,7},... | collective-permute-start | bytes 442376 | tf_op jit(solution)/shard_map/ppermute | solution.py:17
  14.2 0.0 copy-done.4
  14.2 0.0 copy-done.1
  14.2 1.4 %collective-permute-start.2 = (bf16[64,2304]{1,0:T(8,128)(2,1)S(1)}, bf16[64,2304]{1,0:T(8,128)(2,1)S(1)}, u32[]{:S(2)}, u32[]{:S(2)}) collective-permute-start(bf16[64,2304]{1,0:T(8,128)(2,1)S(1)} %pad_maximum_fusion), channel_id=1, source_target_pairs={{0,4},{2,6},{4,0},{6,2},{8,12},{10,14},{12,8},{14,10},{1,5},{3,7},... | collective-permute-start | bytes 884744 | tf_op jit(solution)/shard_map/ppermute | solution.py:17
  15.6 1.6 %collective-permute-start.5 = (bf16[32,2304]{1,0:T(8,128)(2,1)S(1)}, bf16[32,2304]{1,0:T(8,128)(2,1)S(1)}, u32[]{:S(2)}, u32[]{:S(2)}) collective-permute-start(bf16[32,2304]{1,0:T(8,128)(2,1)S(1)} %collective-permute-done.3.rest_2_), channel_id=1, source_target_pairs={{0,16},{16,0},{1,17},{17,1},{2,18},{18,2},{3,19},{19,3},{4,20},{20... | collective-permute-start | bytes 442376 | tf_op jit(solution)/shard_map/ppermute | solution.py:17
  17.2 3.1 %collective-permute-done.4.rest_3_ = bf16[32,2304]{1,0:T(8,128)(2,1)S(1)} collective-permute-done((bf16[32,2304]{1,0:T(8,128)(2,1)S(1)}, bf16[32,2304]{1,0:T(8,128)(2,1)S(1)}, u32[]{:S(2)}, u32[]{:S(2)}) %collective-permute-start.4) | collective-permute-done | bytes 147488 | tf_op jit(solution)/shard_map/ppermute | solution.py:17
  20.3 1.6 %collective-permute-start.6 = (bf16[32,2304]{1,0:T(8,128)(2,1)S(1)}, bf16[32,2304]{1,0:T(8,128)(2,1)S(1)}, u32[]{:S(2)}, u32[]{:S(2)}) collective-permute-start(bf16[32,2304]{1,0:T(8,128)(2,1)S(1)} %collective-permute-done.4.rest_3_), channel_id=1, source_target_pairs={{0,16},{16,0},{1,17},{17,1},{2,18},{18,2},{3,19},{19,3},{4,20},{20... | collective-permute-start | bytes 442376 | tf_op jit(solution)/shard_map/ppermute | solution.py:17
  22.5 0.1 collective-permute-start.8
  22.6 0.0 collective-permute-done.5.rest_4_
  22.6 4.3 %shard_map.132 = (f32[1536,128]{1,0:T(8,128)}, bf16[1536,96]{1,0:T(8,128)(2,1)}) custom-call(s32[96]{0:T(128)} %lengths_ref.1, s32[1]{0:T(128)S(6)} %copy.17.count_ref, bf16[1536,128]{1,0:T(8,128)(2,1)} %bitcast.33, bf16[3072,128]{1,0:T(8,128)(2,1)} %bitcast.31, bf16[192,128]{1,0:T(8,128)(2,1)} %bitcast.34, bf16[3072,128]{1,0:T(8,128)(2,1)} %bitcast.32), custom_call_target="tpu_custom_call" | custom-call | flops 67108864 | bytes 3145728 | tf_op jit(solution)/shard_map/pallas_call | solution.py:120
  26.9 0.0 copy-start.2
  26.9 0.0 copy-start.3
  26.9 0.0 collective-permute-done.6.rest_5_
  26.9 0.0 collective-permute-done.2.rest_1_
  26.9 0.0 collective-permute-done.1.other_ref
  26.9 0.0 copy-done.5
  26.9 0.0 copy-done.6
  26.9 1.1 %shard_map.133.ranks_ref = f32[128,96]{1,0:T(8,128)S(1)} custom-call(s32[8]{0:T(128)S(1)} %copy-done.5, bf16[96,2048]{1,0:T(8,128)(2,1)S(1)} %get-tuple-element.23.rows_ref, bf16[96,2048]{1,0:T(8,128)(2,1)S(1)} %collective-permute-done.1.other_ref, s32[1,96]{1,0:T(1,128)S(1)} %bitcast.29, s32[1,96]{1,0:T(1,128)S(1)} %collective-permute-done.other_adapters_ref.adapters_ref, ...), custom_call_target="tpu_custom_call" | custom-call | tf_op jit(solution)/shard_map/pallas_call | solution.py:307
  28.0 0.6 %collective-permute-start.7 = (f32[128,96]{1,0:T(8,128)S(1)}, f32[128,96]{1,0:T(8,128)S(1)}, u32[]{:S(2)}, u32[]{:S(2)}) collective-permute-start(f32[128,96]{1,0:T(8,128)S(1)} %shard_map.133.ranks_ref), channel_id=1, source_target_pairs={{0,1},{1,0},{2,3},{3,2},{4,5},{5,4},{6,7},{7,6},{8,9},{9,8},{10,11... | collective-permute-start | bytes 147464 | tf_op jit(solution)/shard_map/ppermute | solution.py:17
  28.6 0.9 %collective-permute-done.7.got_ref = f32[128,96]{1,0:T(8,128)S(1)} collective-permute-done((f32[128,96]{1,0:T(8,128)S(1)}, f32[128,96]{1,0:T(8,128)S(1)}, u32[]{:S(2)}, u32[]{:S(2)}) %collective-permute-start.7) | collective-permute-done | bytes 49184 | tf_op jit(solution)/shard_map/ppermute | solution.py:17
  29.5 0.7 %shard_map.134 = (bf16[96,256]{1,0:T(8,128)(2,1)S(1)}, bf16[256,256]{1,0:T(8,128)(2,1)S(1)}) custom-call(s32[8]{0:T(128)S(1)} %copy-done.5, s32[1,96]{1,0:T(1,128)S(1)} %collective-permute-done.other_adapters_ref.adapters_ref, f32[128,96]{1,0:T(8,128)S(1)} %shard_map.133.ranks_ref, f32[128,96]{1,0:T(8,128)S(1)} %collective-permute-done.7.got_ref, ...), custom_call_target="tpu_custom_call" | custom-call | tf_op jit(solution)/shard_map/pallas_call | solution.py:317
  30.2 1.6 %collective-permute-start.9 = (bf16[96,256]{1,0:T(8,128)(2,1)S(1)}, bf16[96,256]{1,0:T(8,128)(2,1)S(1)}, u32[]{:S(2)}, u32[]{:S(2)}) collective-permute-start(bf16[96,256]{1,0:T(8,128)(2,1)S(1)} %get-tuple-element.39), channel_id=1, source_target_pairs={{0,2},{2,0},{4,6},{6,4},{8,10},{10,8},{12,14},{14,12},{1,3},{3,1},... | collective-permute-start | bytes 147464 | tf_op jit(solution)/shard_map/ppermute | solution.py:17
  31.8 0.0 collective-permute-done.8.base_ref
  31.8 0.7 %shard_map.135.own_ref = f32[96,256]{1,0:T(8,128)S(1)} custom-call(s32[8]{0:T(128)S(1)} %copy-done.5, s32[1,96]{1,0:T(1,128)S(1)} %bitcast.30, f32[128,96]{1,0:T(8,128)S(1)} %shard_map.133.ranks_ref, f32[128,96]{1,0:T(8,128)S(1)} %collective-permute-done.7.got_ref, bf16[256,256]{1,0:T(8,128)(2,1)S(1)} %get-tuple-element.36.panel_ref, ...), custom_call_target="tpu_custom_call" | custom-call | tf_op jit(solution)/shard_map/pallas_call | solution.py:329
  32.5 1.8 %collective-permute-done.9.returned_ref = bf16[96,256]{1,0:T(8,128)(2,1)S(1)} collective-permute-done((bf16[96,256]{1,0:T(8,128)(2,1)S(1)}, bf16[96,256]{1,0:T(8,128)(2,1)S(1)}, u32[]{:S(2)}, u32[]{:S(2)}) %collective-permute-start.9) | collective-permute-done | bytes 49184 | tf_op jit(solution)/shard_map/ppermute | solution.py:17
  34.4 0.0 copy-done.2
  34.4 0.0 copy-done.3
  34.4 1.0 %shard_map.136 = (bf16[1536,128]{1,0:T(8,128)(2,1)}, bf16[192,128]{1,0:T(8,128)(2,1)}) custom-call(s32[1]{0:T(128)S(6)} %copy.17.count_ref, f32[96,256]{1,0:T(8,128)S(1)} %shard_map.135.own_ref, bf16[96,256]{1,0:T(8,128)(2,1)S(1)} %collective-permute-done.9.returned_ref, f32[1536,128]{1,0:T(8,128)S(1)} %copy-done.2, bf16[1536,96]{1,0:T(8,128)(2,1)S(1)} %copy-done.3), custom_call_target="tpu_custom_call" | custom-call | tf_op jit(solution)/shard_map/pallas_call | solution.py:185
  (2 shorter events, 0.0 us)
Async XLA Ops:
  0.6 13.6 %copy-start.4 = (bf16[1,64,256]{2,1,0:T(8,128)(2,1)S(1)}, bf16[1,64,256]{2,1,0:T(8,128)(2,1)}, u32[]{:S(2)}) copy-start(bf16[1,64,256]{2,1,0:T(8,128)(2,1)} %param.19) | copy-start | bytes 98308
  0.6 13.6 %copy-start.1 = (bf16[1,64,2048]{2,1,0:T(8,128)(2,1)S(1)}, bf16[1,64,2048]{2,1,0:T(8,128)(2,1)}, u32[]{:S(2)}) copy-start(bf16[1,64,2048]{2,1,0:T(8,128)(2,1)} %param.18) | copy-start | bytes 786436
  2.4 11.1 %collective-permute-start.3 = (bf16[32,2304]{1,0:T(8,128)(2,1)S(1)}, bf16[32,2304]{1,0:T(8,128)(2,1)S(1)}, u32[]{:S(2)}, u32[]{:S(2)}) collective-permute-start(bf16[32,2304]{1,0:T(8,128)(2,1)S(1)} %pad_maximum_fusion.1), channel_id=1, source_target_pairs={{0,8},{2,10},{4,12},{6,14},{8,0},{10,2},{12,4},{14,6},{1,9},{3,11}... | collective-permute-start | bytes 442376 | tf_op jit(solution)/shard_map/ppermute | solution.py:17
  6.5 4.6 %collective-permute-start = (s32[1,96]{1,0:T(1,128)}, s32[1,96]{1,0:T(1,128)S(1)}, u32[]{:S(2)}, u32[]{:S(2)}) collective-permute-start(s32[1,96]{1,0:T(1,128)} %bitcast.28), channel_id=1, source_target_pairs={{0,2},{2,0},{4,6},{6,4},{8,10},{10,8},{12,14},{14,12},{1,3},{3,1},... | collective-permute-start | bytes 1160 | tf_op jit(solution)/shard_map/ppermute | solution.py:17
  8.0 1.6 %copy-start = (bf16[2048,512]{1,0:T(8,128)(2,1)S(1)}, bf16[2048,512]{1,0:T(8,128)(2,1)}, u32[]{:S(2)}) copy-start(bf16[2048,512]{1,0:T(8,128)(2,1)} %weight_ref.1) | copy-start | bytes 6291460
  9.5 17.4 %copy-start.5 = (s32[8]{0:T(128)S(1)}, s32[8]{0:T(128)}, u32[]{:S(2)}) copy-start(s32[8]{0:T(128)} %table_ref.5) | copy-start | bytes 100
  9.5 17.4 %copy-start.6 = (s32[96]{0:T(128)S(1)}, s32[96]{0:T(128)}, u32[]{:S(2)}) copy-start(s32[96]{0:T(128)} %param.20) | copy-start | bytes 1156
  11.1 15.8 %collective-permute-start.1 = (bf16[96,2048]{1,0:T(8,128)(2,1)}, bf16[96,2048]{1,0:T(8,128)(2,1)S(1)}, u32[]{:S(2)}, u32[]{:S(2)}) collective-permute-start(bf16[96,2048]{1,0:T(8,128)(2,1)} %bitcast.1.rows_ref), channel_id=1, source_target_pairs={{0,2},{2,0},{4,6},{6,4},{8,10},{10,8},{12,14},{14,12},{1,3},{3,1},... | collective-permute-start | bytes 1179656 | tf_op jit(solution)/shard_map/ppermute | solution.py:17
  13.5 6.8 %collective-permute-start.4 = (bf16[32,2304]{1,0:T(8,128)(2,1)S(1)}, bf16[32,2304]{1,0:T(8,128)(2,1)S(1)}, u32[]{:S(2)}, u32[]{:S(2)}) collective-permute-start(bf16[32,2304]{1,0:T(8,128)(2,1)S(1)} %collective-permute-done.3.rest_2_), channel_id=1, source_target_pairs={{0,4},{2,6},{4,0},{6,2},{8,12},{10,14},{12,8},{14,10},{1,5},{3,7},... | collective-permute-start | bytes 442376 | tf_op jit(solution)/shard_map/ppermute | solution.py:17
  14.2 12.7 %collective-permute-start.2 = (bf16[64,2304]{1,0:T(8,128)(2,1)S(1)}, bf16[64,2304]{1,0:T(8,128)(2,1)S(1)}, u32[]{:S(2)}, u32[]{:S(2)}) collective-permute-start(bf16[64,2304]{1,0:T(8,128)(2,1)S(1)} %pad_maximum_fusion), channel_id=1, source_target_pairs={{0,4},{2,6},{4,0},{6,2},{8,12},{10,14},{12,8},{14,10},{1,5},{3,7},... | collective-permute-start | bytes 884744 | tf_op jit(solution)/shard_map/ppermute | solution.py:17
  15.6 7.0 %collective-permute-start.5 = (bf16[32,2304]{1,0:T(8,128)(2,1)S(1)}, bf16[32,2304]{1,0:T(8,128)(2,1)S(1)}, u32[]{:S(2)}, u32[]{:S(2)}) collective-permute-start(bf16[32,2304]{1,0:T(8,128)(2,1)S(1)} %collective-permute-done.3.rest_2_), channel_id=1, source_target_pairs={{0,16},{16,0},{1,17},{17,1},{2,18},{18,2},{3,19},{19,3},{4,20},{20... | collective-permute-start | bytes 442376 | tf_op jit(solution)/shard_map/ppermute | solution.py:17
  20.3 6.6 %collective-permute-start.6 = (bf16[32,2304]{1,0:T(8,128)(2,1)S(1)}, bf16[32,2304]{1,0:T(8,128)(2,1)S(1)}, u32[]{:S(2)}, u32[]{:S(2)}) collective-permute-start(bf16[32,2304]{1,0:T(8,128)(2,1)S(1)} %collective-permute-done.4.rest_3_), channel_id=1, source_target_pairs={{0,16},{16,0},{1,17},{17,1},{2,18},{18,2},{3,19},{19,3},{4,20},{20... | collective-permute-start | bytes 442376 | tf_op jit(solution)/shard_map/ppermute | solution.py:17
  22.5 9.3 %collective-permute-start.8 = (f32[96,256]{1,0:T(8,128)S(1)}, f32[96,256]{1,0:T(8,128)S(1)}, u32[]{:S(2)}, u32[]{:S(2)}) collective-permute-start(f32[96,256]{1,0:T(8,128)S(1)} %get-tuple-element.38), channel_id=1, source_target_pairs={{0,1},{1,0},{2,3},{3,2},{4,5},{5,4},{6,7},{7,6},{8,9},{9,8},{10,11... | collective-permute-start | bytes 294920 | tf_op jit(solution)/shard_map/ppermute | solution.py:17
  26.9 7.5 %copy-start.2 = (f32[1536,128]{1,0:T(8,128)S(1)}, f32[1536,128]{1,0:T(8,128)}, u32[]{:S(2)}) copy-start(f32[1536,128]{1,0:T(8,128)} %get-tuple-element.40.rest_0_) | copy-start | bytes 2359300
  26.9 7.5 %copy-start.3 = (bf16[1536,96]{1,0:T(8,128)(2,1)S(1)}, bf16[1536,96]{1,0:T(8,128)(2,1)}, u32[]{:S(2)}) copy-start(bf16[1536,96]{1,0:T(8,128)(2,1)} %get-tuple-element.41.rest_1_) | copy-start | bytes 884740
  28.0 1.5 %collective-permute-start.7 = (f32[128,96]{1,0:T(8,128)S(1)}, f32[128,96]{1,0:T(8,128)S(1)}, u32[]{:S(2)}, u32[]{:S(2)}) collective-permute-start(f32[128,96]{1,0:T(8,128)S(1)} %shard_map.133.ranks_ref), channel_id=1, source_target_pairs={{0,1},{1,0},{2,3},{3,2},{4,5},{5,4},{6,7},{7,6},{8,9},{9,8},{10,11... | collective-permute-start | bytes 147464 | tf_op jit(solution)/shard_map/ppermute | solution.py:17
  30.2 4.2 %collective-permute-start.9 = (bf16[96,256]{1,0:T(8,128)(2,1)S(1)}, bf16[96,256]{1,0:T(8,128)(2,1)S(1)}, u32[]{:S(2)}, u32[]{:S(2)}) collective-permute-start(bf16[96,256]{1,0:T(8,128)(2,1)S(1)} %get-tuple-element.39), channel_id=1, source_target_pairs={{0,2},{2,0},{4,6},{6,4},{8,10},{10,8},{12,14},{14,12},{1,3},{3,1},... | collective-permute-start | bytes 147464 | tf_op jit(solution)/shard_map/ppermute | solution.py:17

commit v4 on v3

--- a/solution.py
+++ b/solution.py
@@ -19,28 +19,7 @@
 
 def cached_kernel(dims, lengths_ref, count_ref, *refs):
     heads, query_heads, context, group, parts, opening, scale = dims
-    sources, outputs, buffers, results = refs[:4], refs[4:6], refs[6:10], refs[10:12]
-    in_sems, out_sems = refs[12:]
-
-    def copy_of(source, target, sem, part):
-        size = min(source.shape[0], target.shape[0]) // parts
-        begin = [(opening + part if ref.shape[0] > size * parts else part) * size for ref in (source, target)]
-        return pltpu.make_async_copy(source.at[pl.ds(begin[0], size)], target.at[pl.ds(begin[1], size)], sem)
-
-    copies = [
-        [copy_of(source, buffer, in_sems.at[part, i], part) for i, (source, buffer) in enumerate(zip(sources, buffers))]
-        for part in range(parts)
-    ]
-    writes = [
-        [copy_of(result, output, out_sems.at[part, i], part) for i, (result, output) in enumerate(zip(results, outputs))]
-        for part in range(parts)
-    ]
-    for group_of_copies in copies:
-        for copy in group_of_copies:
-            copy.start()
-    query_ref, key_ref, fresh_ref, value_ref = buffers
-    mixed_ref, share_ref = results
-
+    query_ref, key_ref, fresh_ref, value_ref, mixed_ref, share_ref = refs
     slots = group // heads
     rows, places = group * query_heads, group * context
     part_rows = query_ref.shape[0] // parts
@@ -57,8 +36,6 @@
     row_slot = lax.broadcasted_iota(jnp.int32, (part_rows, 1), 0) // (heads * query_heads)
     lane = lax.broadcasted_iota(jnp.int32, (1, places), 1)
     for part in range(parts):
-        for copy in copies[part]:
-            copy.wait()
         query = query_ref[pl.ds(part * part_rows, part_rows), :]
         fresh_keys = fresh_ref[pl.ds(part * part_pairs, part_pairs), :]
         fresh = lax.dot_general(query, fresh_keys, contract, preferred_element_type=jnp.float32) * scale
@@ -92,11 +69,6 @@
         mixed_ref[pl.ds(part * part_rows, part_rows), :] = jnp.concatenate(mixed, axis=0)
         share = jnp.where(own_fresh, fresh_share * inverse, 0.0)
         share_ref[pl.ds(part * part_rows, part_rows), :] = share.astype(share_ref.dtype)
-        for write in writes[part]:
-            write.start()
-    for group_of_writes in writes:
-        for write in group_of_writes:
-            write.wait()
 
 
 def cached_attention(opening, parts, query_rows, fresh_keys, cached_keys, cached_values, lengths, live_count):
@@ -117,15 +89,13 @@
         jax.ShapeDtypeStruct((rows, pairs // runs), jnp.bfloat16),
     ]
     smem = pl.BlockSpec(memory_space=pltpu.SMEM)
+    vmem = pl.BlockSpec(memory_space=pltpu.VMEM)
     return pl.pallas_call(
         functools.partial(cached_kernel, dims),
-        in_specs=[smem, smem] + [pl.BlockSpec(memory_space=pl.ANY)] * len(inputs),
-        out_specs=[pl.BlockSpec(memory_space=pl.ANY)] * 2,
+        in_specs=[smem, smem] + [vmem] * len(inputs),
+        out_specs=[vmem] * 2,
         out_shape=outputs,
-        scratch_shapes=[pltpu.VMEM((x.shape[0] // runs * parts, x.shape[1]), x.dtype) for x in inputs]
-        + [pltpu.VMEM(x.shape, x.dtype) for x in outputs]
-        + [pltpu.SemaphoreType.DMA((parts, len(inputs))), pltpu.SemaphoreType.DMA((parts, len(outputs)))],
-        compiler_params=pltpu.CompilerParams(vmem_limit_bytes=56 << 20),
+        compiler_params=pltpu.CompilerParams(vmem_limit_bytes=16 << 20),
         cost_estimate=pl.CostEstimate(flops=1 << 26, bytes_accessed=3 << 20, transcendentals=1 << 17),
     )(lengths, live_count, *inputs)
 
@@ -285,13 +255,13 @@
     other_adapters, sent_rows, base_sent = lax.optimization_barrier((swap(adapters, "replica", 1), rows, base_sent))
     other = swap(sent_rows, "replica", 1)
     near = swap(jnp.concatenate([down, up], axis=1), "replica", 2)
-    query_rows, *attention_rest = attention_inputs
+    *attention_arrays, lengths, live_count = attention_inputs
     held = [(0, packed)]
     bit = replicas // 4
     while bit:
         came = [(offset ^ bit, swap(part, "replica", 2 * bit)) for offset, part in held if offset or bit > 1]
         if len(held) == 1:
-            first, base_sent, query_rows = lax.optimization_barrier((came[0][1], base_sent, query_rows))
+            first, base_sent = lax.optimization_barrier((came[0][1], base_sent))
             came = [(came[0][0], first)]
         held = held + came
         bit //= 2
@@ -299,8 +269,8 @@
     offsets = [0, 1] + [offset for offset, _ in held[1:]]
     mine = [part for _, part in held[1:]]
     theirs = [swap(part, "group", 1) for part in mine]
-    mine[-1], theirs[-2], query_rows = lax.optimization_barrier((mine[-1], theirs[-2], query_rows))
-    halves = cached_attention(0, 2, query_rows, *attention_rest)
+    mine[-1], theirs[-2], lengths = lax.optimization_barrier((mine[-1], theirs[-2], lengths))
+    halves = cached_attention(0, 2, *attention_arrays, lengths, live_count)
 
     theirs[-1], halves = lax.optimization_barrier((theirs[-1], halves))
     inputs = [rows_near, other, adapters, other_adapters, down, near] + mine + theirs

time: 35.7 us -> 34 us (0.952)
  Pallas kernels: 9.38 us -> 7.12 us
  waiting for transfers between devices: 7.65 us -> 8.68 us
  starting transfers between devices: 13.6 us -> 13.2 us
    pallas_call x1, Pallas kernels: 4.28 us -> 1.9 us  [cached_attention(): pl.pallas_call(functools.partial(cached_kernel, dims), in_specs=[smem, sm...]
    ppermute x10, waiting for transfers between devices: 7.65 us -> 8.68 us  [swap(): return lax.ppermute(array, axis, [(i, i ^ bit) for i in range(size)])]
    ppermute x10, starting transfers between devices: 13.6 us -> 13.2 us  [swap(): return lax.ppermute(array, axis, [(i, i ^ bit) for i in range(size)])]
    unnamed x14 -> x20, local copies, waits for them, and re-layouts: 1.62 us -> 1.63 us
  transfers between devices with their start and end apart: 10 -> 10, of which waited for: 4 -> 5; matrix products, arithmetic and copies ran while one was open for 0% -> 0% of each run, Pallas kernels for 24% -> 18%
where the time goes in v4:
time: 34 us; the launch traced here: 33.8 us
  starting transfers between devices  13.2 us (39%)
  waiting for transfers between devices  8.68 us (26%)
  Pallas kernels  7.12 us (21%)
  local copies, waits for them, and re-layouts  3.3 us (10%)
  between operations  1.47 us (4%)
    ppermute x10, starting transfers between devices, swap(): return lax.ppermute(array, axis, [(i, i ^ bit) for i in range(size)])  13.2 us
    ppermute x10, waiting for transfers between devices, swap(): return lax.ppermute(array, axis, [(i, i ^ bit) for i in range(size)])  8.68 us
    pallas_call x1, Pallas kernels, cached_attention(): pl.pallas_call(functools.partial(cached_kernel, dims), in_specs=[smem, sm...  1.9 us
    unnamed x20, local copies, waits for them, and re-layouts  1.63 us
    pallas_call x1, Pallas kernels, base_sums(): pl.pallas_call(base_kernel, in_specs=[vmem, vmem], out_specs=[vmem, vmem,...  1.62 us
    pallas_call x1, Pallas kernels, gathered_values(): pl.pallas_call(functools.partial(rank_kernel, offsets, half, (2, len(mine...  1.1 us
    pallas_call x1, Pallas kernels, finish(): pl.pallas_call(final_kernel, in_specs=[pl.BlockSpec(memory_space=pltpu.SM...  1.02 us
    dynamic_slice x1, local copies, waits for them, and re-layouts, gathered_values(): lax.dynamic_slice_in_dim(down, start, half, 0)  0.91 us
  transfers between devices with their start and end apart: 10, of which 5 were waited for; matrix products, arithmetic and copies ran while one was open for 0% of the time, Pallas kernels for 18%

profile of v4, /device:TPU:0, one launch (start us, length us, event | category | flops | bytes accessed | tf_op | source)
XLA Modules:
  0.0 33.8 jit_solution(11000477724865131476)
XLA Ops:
  0.6 0.0 copy-start.5
  0.6 0.0 copy-start.1
  0.7 0.0 copy-start.9
  0.7 0.0 copy-start.6
  0.7 0.8 %dynamic-slice_bitcast_fusion.1 = bf16[32,256]{1,0:T(8,128)(2,1)S(1)} fusion(bf16[1,64,256]{2,1,0:T(8,128)(2,1)} %param.19, s32[]{:T(128)S(6)} %select_n.4), kind=kLoop, calls=%fused_computation.3 | loop fusion | bytes 32772 | tf_op jit(solution)/shard_map/dynamic_slice | solution.py:252
  1.4 0.9 %dynamic-slice_bitcast_fusion = bf16[32,2048]{1,0:T(8,128)(2,1)S(1)} fusion(bf16[1,64,2048]{2,1,0:T(8,128)(2,1)} %param.18, s32[]{:T(128)S(6)} %select_n.4), kind=kLoop, calls=%fused_computation.2 | loop fusion | bytes 262148 | tf_op jit(solution)/shard_map/dynamic_slice | solution.py:252
  2.4 4.1 %collective-permute-start.3 = (bf16[32,2304]{1,0:T(8,128)(2,1)S(1)}, bf16[32,2304]{1,0:T(8,128)(2,1)S(1)}, u32[]{:S(2)}, u32[]{:S(2)}) collective-permute-start(bf16[32,2304]{1,0:T(8,128)(2,1)S(1)} %pad_maximum_fusion.1), channel_id=1, source_target_pairs={{0,8},{2,10},{4,12},{6,14},{8,0},{10,2},{12,4},{14,6},{1,9},{3,11}... | collective-permute-start | bytes 442376 | tf_op jit(solution)/shard_map/ppermute | solution.py:17
  6.5 1.5 %collective-permute-start = (s32[1,96]{1,0:T(1,128)}, s32[1,96]{1,0:T(1,128)S(1)}, u32[]{:S(2)}, u32[]{:S(2)}) collective-permute-start(s32[1,96]{1,0:T(1,128)} %bitcast.32), channel_id=1, source_target_pairs={{0,2},{2,0},{4,6},{6,4},{8,10},{10,8},{12,14},{14,12},{1,3},{3,1},... | collective-permute-start | bytes 1160 | tf_op jit(solution)/shard_map/ppermute | solution.py:17
  8.0 0.0 copy-start
  8.0 1.6 %copy-done = bf16[2048,512]{1,0:T(8,128)(2,1)S(1)} copy-done((bf16[2048,512]{1,0:T(8,128)(2,1)S(1)}, bf16[2048,512]{1,0:T(8,128)(2,1)}, u32[]{:S(2)}) %copy-start) | copy-done | bytes 2097176
  9.6 0.0 copy-start.2
  9.6 0.0 copy-start.3
  9.6 0.0 copy-start.4
  9.6 0.0 copy-start.7
  9.6 0.0 copy-start.8
  9.6 1.6 %shard_map.131 = (f32[96,256]{1,0:T(8,128)S(1)}, f32[96,256]{1,0:T(8,128)S(1)}, bf16[96,2048]{1,0:T(8,128)(2,1)S(1)}) custom-call(bf16[96,2048]{1,0:T(8,128)(2,1)} %bitcast.1.rows_ref, bf16[2048,512]{1,0:T(8,128)(2,1)S(1)} %copy-done), custom_call_target="tpu_custom_call" | custom-call | flops 268435456 | bytes 3145728 | tf_op jit(solution)/shard_map/pallas_call | solution.py:115
  11.2 0.0 collective-permute-done.other_adapters_ref.adapters_ref
  11.2 0.6 %collective-permute-start.1 = (bf16[96,2048]{1,0:T(8,128)(2,1)}, bf16[96,2048]{1,0:T(8,128)(2,1)S(1)}, u32[]{:S(2)}, u32[]{:S(2)}) collective-permute-start(bf16[96,2048]{1,0:T(8,128)(2,1)} %bitcast.1.rows_ref), channel_id=1, source_target_pairs={{0,2},{2,0},{4,6},{6,4},{8,10},{10,8},{12,14},{14,12},{1,3},{3,1},... | collective-permute-start | bytes 1179656 | tf_op jit(solution)/shard_map/ppermute | solution.py:17
  11.8 1.7 %collective-permute-done.3.rest_2_ = bf16[32,2304]{1,0:T(8,128)(2,1)S(1)} collective-permute-done((bf16[32,2304]{1,0:T(8,128)(2,1)S(1)}, bf16[32,2304]{1,0:T(8,128)(2,1)S(1)}, u32[]{:S(2)}, u32[]{:S(2)}) %collective-permute-start.3) | collective-permute-done | bytes 147488 | tf_op jit(solution)/shard_map/ppermute | solution.py:17
  13.5 0.7 %collective-permute-start.4 = (bf16[32,2304]{1,0:T(8,128)(2,1)S(1)}, bf16[32,2304]{1,0:T(8,128)(2,1)S(1)}, u32[]{:S(2)}, u32[]{:S(2)}) collective-permute-start(bf16[32,2304]{1,0:T(8,128)(2,1)S(1)} %collective-permute-done.3.rest_2_), channel_id=1, source_target_pairs={{0,4},{2,6},{4,0},{6,2},{8,12},{10,14},{12,8},{14,10},{1,5},{3,7},... | collective-permute-start | bytes 442376 | tf_op jit(solution)/shard_map/ppermute | solution.py:17
  14.2 0.0 copy-done.5
  14.2 0.0 copy-done.1
  14.2 1.4 %collective-permute-start.2 = (bf16[64,2304]{1,0:T(8,128)(2,1)S(1)}, bf16[64,2304]{1,0:T(8,128)(2,1)S(1)}, u32[]{:S(2)}, u32[]{:S(2)}) collective-permute-start(bf16[64,2304]{1,0:T(8,128)(2,1)S(1)} %pad_maximum_fusion), channel_id=1, source_target_pairs={{0,4},{2,6},{4,0},{6,2},{8,12},{10,14},{12,8},{14,10},{1,5},{3,7},... | collective-permute-start | bytes 884744 | tf_op jit(solution)/shard_map/ppermute | solution.py:17
  15.6 1.6 %collective-permute-start.5 = (bf16[32,2304]{1,0:T(8,128)(2,1)S(1)}, bf16[32,2304]{1,0:T(8,128)(2,1)S(1)}, u32[]{:S(2)}, u32[]{:S(2)}) collective-permute-start(bf16[32,2304]{1,0:T(8,128)(2,1)S(1)} %collective-permute-done.3.rest_2_), channel_id=1, source_target_pairs={{0,16},{16,0},{1,17},{17,1},{2,18},{18,2},{3,19},{19,3},{4,20},{20... | collective-permute-start | bytes 442376 | tf_op jit(solution)/shard_map/ppermute | solution.py:17
  17.2 3.1 %collective-permute-done.4.rest_3_ = bf16[32,2304]{1,0:T(8,128)(2,1)S(1)} collective-permute-done((bf16[32,2304]{1,0:T(8,128)(2,1)S(1)}, bf16[32,2304]{1,0:T(8,128)(2,1)S(1)}, u32[]{:S(2)}, u32[]{:S(2)}) %collective-permute-start.4) | collective-permute-done | bytes 147488 | tf_op jit(solution)/shard_map/ppermute | solution.py:17
  20.3 1.6 %collective-permute-start.6 = (bf16[32,2304]{1,0:T(8,128)(2,1)S(1)}, bf16[32,2304]{1,0:T(8,128)(2,1)S(1)}, u32[]{:S(2)}, u32[]{:S(2)}) collective-permute-start(bf16[32,2304]{1,0:T(8,128)(2,1)S(1)} %collective-permute-done.4.rest_3_), channel_id=1, source_target_pairs={{0,16},{16,0},{1,17},{17,1},{2,18},{18,2},{3,19},{19,3},{4,20},{20... | collective-permute-start | bytes 442376 | tf_op jit(solution)/shard_map/ppermute | solution.py:17
  22.5 0.1 collective-permute-start.8
  22.6 0.0 collective-permute-done.5.rest_4_
  22.6 0.0 copy-done.9
  22.6 0.0 copy-done.6
  22.6 0.0 copy-done.2
  22.6 0.0 copy-done.3
  22.6 0.0 copy-done.4
  22.6 1.9 %shard_map.132 = (f32[1536,128]{1,0:T(8,128)S(1)}, bf16[1536,96]{1,0:T(8,128)(2,1)S(1)}) custom-call(s32[96]{0:T(128)S(1)} %copy-done.9, s32[1]{0:T(128)S(6)} %copy.17.count_ref, bf16[1536,128]{1,0:T(8,128)(2,1)S(1)} %bitcast.28, bf16[3072,128]{1,0:T(8,128)(2,1)S(1)} %bitcast.26, bf16[192,128]{1,0:T(8,128)(2,1)S(1)} %bitcast.31, bf16[3072,128]{1,0:T(8,128)(2,1)S(1)} %bitcast.27), custom_call_target="tpu_custom_call" | custom-call | flops 67108864 | bytes 3145728 | tf_op jit(solution)/shard_map/pallas_call | solution.py:93
  24.5 0.9 %collective-permute-done.6.rest_5_ = bf16[32,2304]{1,0:T(8,128)(2,1)S(1)} collective-permute-done((bf16[32,2304]{1,0:T(8,128)(2,1)S(1)}, bf16[32,2304]{1,0:T(8,128)(2,1)S(1)}, u32[]{:S(2)}, u32[]{:S(2)}) %collective-permute-start.6) | collective-permute-done | bytes 147488 | tf_op jit(solution)/shard_map/ppermute | solution.py:17
  25.4 0.0 collective-permute-done.2.rest_1_
  25.4 0.0 collective-permute-done.1.other_ref
  25.4 0.0 copy-done.7
  25.4 0.0 copy-done.8
  25.4 1.1 %shard_map.133.ranks_ref = f32[128,96]{1,0:T(8,128)S(1)} custom-call(s32[8]{0:T(128)S(1)} %copy-done.7, bf16[96,2048]{1,0:T(8,128)(2,1)S(1)} %get-tuple-element.22.rows_ref, bf16[96,2048]{1,0:T(8,128)(2,1)S(1)} %collective-permute-done.1.other_ref, s32[1,96]{1,0:T(1,128)S(1)} %bitcast.33, s32[1,96]{1,0:T(1,128)S(1)} %collective-permute-done.other_adapters_ref.adapters_ref, ...), custom_call_target="tpu_custom_call" | custom-call | tf_op jit(solution)/shard_map/pallas_call | solution.py:277
  26.5 0.1 collective-permute-start.7
  26.6 1.2 %collective-permute-done.7.got_ref = f32[128,96]{1,0:T(8,128)S(1)} collective-permute-done((f32[128,96]{1,0:T(8,128)S(1)}, f32[128,96]{1,0:T(8,128)S(1)}, u32[]{:S(2)}, u32[]{:S(2)}) %collective-permute-start.7) | collective-permute-done | bytes 49184 | tf_op jit(solution)/shard_map/ppermute | solution.py:17
  27.9 0.7 %shard_map.134 = (bf16[96,256]{1,0:T(8,128)(2,1)S(1)}, bf16[256,256]{1,0:T(8,128)(2,1)S(1)}) custom-call(s32[8]{0:T(128)S(1)} %copy-done.7, s32[1,96]{1,0:T(1,128)S(1)} %collective-permute-done.other_adapters_ref.adapters_ref, f32[128,96]{1,0:T(8,128)S(1)} %shard_map.133.ranks_ref, f32[128,96]{1,0:T(8,128)S(1)} %collective-permute-done.7.got_ref, ...), custom_call_target="tpu_custom_call" | custom-call | tf_op jit(solution)/shard_map/pallas_call | solution.py:287
  28.6 1.6 %collective-permute-start.9 = (bf16[96,256]{1,0:T(8,128)(2,1)S(1)}, bf16[96,256]{1,0:T(8,128)(2,1)S(1)}, u32[]{:S(2)}, u32[]{:S(2)}) collective-permute-start(bf16[96,256]{1,0:T(8,128)(2,1)S(1)} %get-tuple-element.37), channel_id=1, source_target_pairs={{0,2},{2,0},{4,6},{6,4},{8,10},{10,8},{12,14},{14,12},{1,3},{3,1},... | collective-permute-start | bytes 147464 | tf_op jit(solution)/shard_map/ppermute | solution.py:17
  30.2 0.0 collective-permute-done.8.base_ref
  30.2 0.7 %shard_map.135.own_ref = f32[96,256]{1,0:T(8,128)S(1)} custom-call(s32[8]{0:T(128)S(1)} %copy-done.7, s32[1,96]{1,0:T(1,128)S(1)} %bitcast.34, f32[128,96]{1,0:T(8,128)S(1)} %shard_map.133.ranks_ref, f32[128,96]{1,0:T(8,128)S(1)} %collective-permute-done.7.got_ref, bf16[256,256]{1,0:T(8,128)(2,1)S(1)} %get-tuple-element.34.panel_ref, ...), custom_call_target="tpu_custom_call" | custom-call | tf_op jit(solution)/shard_map/pallas_call | solution.py:299
  31.0 1.8 %collective-permute-done.9.returned_ref = bf16[96,256]{1,0:T(8,128)(2,1)S(1)} collective-permute-done((bf16[96,256]{1,0:T(8,128)(2,1)S(1)}, bf16[96,256]{1,0:T(8,128)(2,1)S(1)}, u32[]{:S(2)}, u32[]{:S(2)}) %collective-permute-start.9) | collective-permute-done | bytes 49184 | tf_op jit(solution)/shard_map/ppermute | solution.py:17
  32.8 1.0 %shard_map.136 = (bf16[1536,128]{1,0:T(8,128)(2,1)}, bf16[192,128]{1,0:T(8,128)(2,1)}) custom-call(s32[1]{0:T(128)S(6)} %copy.17.count_ref, f32[96,256]{1,0:T(8,128)S(1)} %shard_map.135.own_ref, bf16[96,256]{1,0:T(8,128)(2,1)S(1)} %collective-permute-done.9.returned_ref, f32[1536,128]{1,0:T(8,128)S(1)} %get-tuple-element.38.rest_0_, ...), custom_call_target="tpu_custom_call" | custom-call | tf_op jit(solution)/shard_map/pallas_call | solution.py:155
  (2 shorter events, 0.0 us)
Async XLA Ops:
  0.6 13.6 %copy-start.5 = (bf16[1,64,256]{2,1,0:T(8,128)(2,1)S(1)}, bf16[1,64,256]{2,1,0:T(8,128)(2,1)}, u32[]{:S(2)}) copy-start(bf16[1,64,256]{2,1,0:T(8,128)(2,1)} %param.19) | copy-start | bytes 98308
  0.6 13.6 %copy-start.1 = (bf16[1,64,2048]{2,1,0:T(8,128)(2,1)S(1)}, bf16[1,64,2048]{2,1,0:T(8,128)(2,1)}, u32[]{:S(2)}) copy-start(bf16[1,64,2048]{2,1,0:T(8,128)(2,1)} %param.18) | copy-start | bytes 786436
  0.7 21.9 %copy-start.9 = (s32[96]{0:T(128)S(1)}, s32[96]{0:T(128)}, u32[]{:S(2)}) copy-start(s32[96]{0:T(128)} %lengths_ref) | copy-start | bytes 1156
  0.7 21.9 %copy-start.6 = (bf16[96,1,2,128]{3,2,1,0:T(2,128)(2,1)S(1)}, bf16[96,1,2,128]{3,2,1,0:T(2,128)(2,1)}, u32[]{:S(2)}) copy-start(bf16[96,1,2,128]{3,2,1,0:T(2,128)(2,1)} %param.14) | copy-start | bytes 147460
  2.4 11.1 %collective-permute-start.3 = (bf16[32,2304]{1,0:T(8,128)(2,1)S(1)}, bf16[32,2304]{1,0:T(8,128)(2,1)S(1)}, u32[]{:S(2)}, u32[]{:S(2)}) collective-permute-start(bf16[32,2304]{1,0:T(8,128)(2,1)S(1)} %pad_maximum_fusion.1), channel_id=1, source_target_pairs={{0,8},{2,10},{4,12},{6,14},{8,0},{10,2},{12,4},{14,6},{1,9},{3,11}... | collective-permute-start | bytes 442376 | tf_op jit(solution)/shard_map/ppermute | solution.py:17
  6.5 4.7 %collective-permute-start = (s32[1,96]{1,0:T(1,128)}, s32[1,96]{1,0:T(1,128)S(1)}, u32[]{:S(2)}, u32[]{:S(2)}) collective-permute-start(s32[1,96]{1,0:T(1,128)} %bitcast.32), channel_id=1, source_target_pairs={{0,2},{2,0},{4,6},{6,4},{8,10},{10,8},{12,14},{14,12},{1,3},{3,1},... | collective-permute-start | bytes 1160 | tf_op jit(solution)/shard_map/ppermute | solution.py:17
  8.0 1.6 %copy-start = (bf16[2048,512]{1,0:T(8,128)(2,1)S(1)}, bf16[2048,512]{1,0:T(8,128)(2,1)}, u32[]{:S(2)}) copy-start(bf16[2048,512]{1,0:T(8,128)(2,1)} %weight_ref.1) | copy-start | bytes 6291460
  9.6 13.0 %copy-start.2 = (bf16[96,2,16,128]{3,2,1,0:T(8,128)(2,1)S(1)}, bf16[96,2,16,128]{3,2,1,0:T(8,128)(2,1)}, u32[]{:S(2)}) copy-start(bf16[96,2,16,128]{3,2,1,0:T(8,128)(2,1)} %param.15) | copy-start | bytes 2359300
  9.6 13.1 %copy-start.3 = (bf16[96,2,16,128]{3,2,1,0:T(8,128)(2,1)S(1)}, bf16[96,2,16,128]{3,2,1,0:T(8,128)(2,1)}, u32[]{:S(2)}) copy-start(bf16[96,2,16,128]{3,2,1,0:T(8,128)(2,1)} %param.16) | copy-start | bytes 2359300
  9.6 13.1 %copy-start.4 = (bf16[96,1,2,1024]{3,2,1,0:T(2,128)(2,1)S(1)}, bf16[96,1,2,1024]{3,2,1,0:T(2,128)(2,1)}, u32[]{:S(2)}) copy-start(bf16[96,1,2,1024]{3,2,1,0:T(2,128)(2,1)} %param.13) | copy-start | bytes 1179652
  9.6 15.9 %copy-start.7 = (s32[8]{0:T(128)S(1)}, s32[8]{0:T(128)}, u32[]{:S(2)}) copy-start(s32[8]{0:T(128)} %table_ref.5) | copy-start | bytes 100
  9.6 15.9 %copy-start.8 = (s32[96]{0:T(128)S(1)}, s32[96]{0:T(128)}, u32[]{:S(2)}) copy-start(s32[96]{0:T(128)} %param.20) | copy-start | bytes 1156
  11.2 14.2 %collective-permute-start.1 = (bf16[96,2048]{1,0:T(8,128)(2,1)}, bf16[96,2048]{1,0:T(8,128)(2,1)S(1)}, u32[]{:S(2)}, u32[]{:S(2)}) collective-permute-start(bf16[96,2048]{1,0:T(8,128)(2,1)} %bitcast.1.rows_ref), channel_id=1, source_target_pairs={{0,2},{2,0},{4,6},{6,4},{8,10},{10,8},{12,14},{14,12},{1,3},{3,1},... | collective-permute-start | bytes 1179656 | tf_op jit(solution)/shard_map/ppermute | solution.py:17
  13.5 6.8 %collective-permute-start.4 = (bf16[32,2304]{1,0:T(8,128)(2,1)S(1)}, bf16[32,2304]{1,0:T(8,128)(2,1)S(1)}, u32[]{:S(2)}, u32[]{:S(2)}) collective-permute-start(bf16[32,2304]{1,0:T(8,128)(2,1)S(1)} %collective-permute-done.3.rest_2_), channel_id=1, source_target_pairs={{0,4},{2,6},{4,0},{6,2},{8,12},{10,14},{12,8},{14,10},{1,5},{3,7},... | collective-permute-start | bytes 442376 | tf_op jit(solution)/shard_map/ppermute | solution.py:17
  14.2 11.2 %collective-permute-start.2 = (bf16[64,2304]{1,0:T(8,128)(2,1)S(1)}, bf16[64,2304]{1,0:T(8,128)(2,1)S(1)}, u32[]{:S(2)}, u32[]{:S(2)}) collective-permute-start(bf16[64,2304]{1,0:T(8,128)(2,1)S(1)} %pad_maximum_fusion), channel_id=1, source_target_pairs={{0,4},{2,6},{4,0},{6,2},{8,12},{10,14},{12,8},{14,10},{1,5},{3,7},... | collective-permute-start | bytes 884744 | tf_op jit(solution)/shard_map/ppermute | solution.py:17
  15.6 7.0 %collective-permute-start.5 = (bf16[32,2304]{1,0:T(8,128)(2,1)S(1)}, bf16[32,2304]{1,0:T(8,128)(2,1)S(1)}, u32[]{:S(2)}, u32[]{:S(2)}) collective-permute-start(bf16[32,2304]{1,0:T(8,128)(2,1)S(1)} %collective-permute-done.3.rest_2_), channel_id=1, source_target_pairs={{0,16},{16,0},{1,17},{17,1},{2,18},{18,2},{3,19},{19,3},{4,20},{20... | collective-permute-start | bytes 442376 | tf_op jit(solution)/shard_map/ppermute | solution.py:17
  20.3 5.1 %collective-permute-start.6 = (bf16[32,2304]{1,0:T(8,128)(2,1)S(1)}, bf16[32,2304]{1,0:T(8,128)(2,1)S(1)}, u32[]{:S(2)}, u32[]{:S(2)}) collective-permute-start(bf16[32,2304]{1,0:T(8,128)(2,1)S(1)} %collective-permute-done.4.rest_3_), channel_id=1, source_target_pairs={{0,16},{16,0},{1,17},{17,1},{2,18},{18,2},{3,19},{19,3},{4,20},{20... | collective-permute-start | bytes 442376 | tf_op jit(solution)/shard_map/ppermute | solution.py:17
  22.5 7.7 %collective-permute-start.8 = (f32[96,256]{1,0:T(8,128)S(1)}, f32[96,256]{1,0:T(8,128)S(1)}, u32[]{:S(2)}, u32[]{:S(2)}) collective-permute-start(f32[96,256]{1,0:T(8,128)S(1)} %get-tuple-element.36), channel_id=1, source_target_pairs={{0,1},{1,0},{2,3},{3,2},{4,5},{5,4},{6,7},{7,6},{8,9},{9,8},{10,11... | collective-permute-start | bytes 294920 | tf_op jit(solution)/shard_map/ppermute | solution.py:17
  26.5 1.3 %collective-permute-start.7 = (f32[128,96]{1,0:T(8,128)S(1)}, f32[128,96]{1,0:T(8,128)S(1)}, u32[]{:S(2)}, u32[]{:S(2)}) collective-permute-start(f32[128,96]{1,0:T(8,128)S(1)} %shard_map.133.ranks_ref), channel_id=1, source_target_pairs={{0,1},{1,0},{2,3},{3,2},{4,5},{5,4},{6,7},{7,6},{8,9},{9,8},{10,11... | collective-permute-start | bytes 147464 | tf_op jit(solution)/shard_map/ppermute | solution.py:17
  28.6 4.2 %collective-permute-start.9 = (bf16[96,256]{1,0:T(8,128)(2,1)S(1)}, bf16[96,256]{1,0:T(8,128)(2,1)S(1)}, u32[]{:S(2)}, u32[]{:S(2)}) collective-permute-start(bf16[96,256]{1,0:T(8,128)(2,1)S(1)} %get-tuple-element.37), channel_id=1, source_target_pairs={{0,2},{2,0},{4,6},{6,4},{8,10},{10,8},{12,14},{14,12},{1,3},{3,1},... | collective-permute-start | bytes 147464 | tf_op jit(solution)/shard_map/ppermute | solution.py:17
